TPU v7x, 128 devices: a whole 4x4x4 slice. The times are simulated.
128 devices in a mesh: tm: 16 (over y, x_hi, core), dp: 8 (over x_lo, z).
Axes of the slice: x: 4 (x_hi: 2, x_lo: 2; x = x_hi * 2 + x_lo), y: 4, z: 4, core: 2. Of those that a mesh axis runs over, the one named last changes fastest.
Arguments:
- queries: bfloat16 [8, 12288, 1536], P('dp', 'tm'), may hold values from -256 to 256
- key_states: bfloat16 [8, 12288, 1536], P('dp', 'tm'), may hold values from -4 to 4
- value_states: bfloat16 [8, 12288, 1536], P('dp', 'tm'), may hold values from -6 to 6
- out_grad: bfloat16 [8, 12288, 1536], P('dp', 'tm'), may hold values from -12 to 12
- out_weight: bfloat16 [1536, 1536], P('dp'), may hold values from -0.15625 to 0.15625
- win_time: int32 [8, 32, 3], P('dp', 'tm'), may hold values from -1 to 1, as said below
- win_space: int32 [8, 32, 3], P('dp', 'tm'), may hold values from 0 to 1
- tile_len: int32 [8, 32], P('dp'), may hold values from 192 to 384, as said below
Outputs:
- query_grad: bfloat16 [8, 12288, 1536], P('dp', 'tm')
- key_grad: bfloat16 [8, 12288, 1536], P('dp', 'tm')
- value_grad: bfloat16 [8, 12288, 1536], P('dp', 'tm')
- weight_grad: float32 [1536, 1536], P(('tm', 'dp'))
Inputs may be any that keep to these rules, and one draw needn't show every extreme that they name: `win_time`: the 3 tiles that a query tile's further slots name are distinct and never the query tile itself; the offset counts slabs along the loop of 16 slabs. `tile_len`: the valid tokens are the first ones of the tile.
All inputs are finite; a program needn't handle non-finite values.
Results may differ from a plain program's by a relative error of at most 0.015.
Values may be sent and summed in bfloat16 or wider, within the bound.
No kernel may reach another device: no remote copies, remote signals or barrier semaphores. Data moves between devices by JAX's collectives and lax.ppermute only.
A program may use at most 192 MiB of HBM per device.

v0:
```python
import math

import jax
import jax.numpy as jnp
from jax import lax
from jax.sharding import PartitionSpec as P

HEAD = 128
TILE = 384


def passed_along(array, axis, by):
    size = lax.axis_size(axis)
    return lax.ppermute(array, axis, [(i, (i + by) % size) for i in range(size)])


def slab_grads(query_tiles, dout_tiles, pool_key, pool_value, pool_len, slot_codes):
    tile_count, tile_size, features = query_tiles.shape
    pool_count = pool_key.shape[0]
    slot_count = slot_codes.shape[1]
    head_count = features // HEAD
    scaling = 1.0 / math.sqrt(HEAD)
    select = slot_codes[:, :, None] == lax.broadcasted_iota(
        jnp.int32, (tile_count, slot_count, pool_count), 2
    )
    lengths = jnp.sum(jnp.where(select, pool_len[None, None, :], 0), axis=2)
    usable = (
        lax.broadcasted_iota(jnp.int32, (tile_count, slot_count, tile_size), 2)
        < lengths[:, :, None]
    )
    usable = usable.reshape(tile_count, 1, slot_count * tile_size)
    flat_codes = slot_codes.reshape(-1)
    window_key = jnp.take(pool_key, flat_codes, axis=0).reshape(
        tile_count, slot_count * tile_size, head_count, HEAD
    )
    window_value = jnp.take(pool_value, flat_codes, axis=0).reshape(
        tile_count, slot_count * tile_size, head_count, HEAD
    )
    select_f = select.astype(jnp.float32)

    def per_head(stacked):
        query_head, dout_head, key_head, value_head = stacked
        scores = (
            jnp.einsum("tqd,tkd->tqk", query_head, key_head, preferred_element_type=jnp.float32)
            * scaling
        )
        scores = jnp.where(usable, scores, -jnp.inf)
        row_max = jnp.max(scores, axis=2, keepdims=True)
        exponent = jnp.exp(scores - row_max)
        probs_f = exponent / jnp.sum(exponent, axis=2, keepdims=True)
        weights = probs_f.astype(jnp.bfloat16)
        attended = jnp.einsum(
            "tqk,tkd->tqd", weights, value_head, preferred_element_type=jnp.float32
        ).astype(jnp.bfloat16)
        attended = lax.optimization_barrier(attended)
        prob_grad = jnp.einsum(
            "tqd,tkd->tqk", dout_head, value_head, preferred_element_type=jnp.float32
        )
        rowdot = jnp.sum(
            dout_head.astype(jnp.float32) * attended.astype(jnp.float32), axis=2, keepdims=True
        )
        dscore = (probs_f * (prob_grad - rowdot)).astype(jnp.bfloat16)
        query_out = (
            jnp.einsum("tqk,tkd->tqd", dscore, key_head, preferred_element_type=jnp.float32)
            * scaling
        ).astype(jnp.bfloat16)
        key_part = (
            jnp.einsum("tqk,tqd->tkd", dscore, query_head, preferred_element_type=jnp.float32)
            * scaling
        )
        value_part = jnp.einsum(
            "tqk,tqd->tkd", weights, dout_head, preferred_element_type=jnp.float32
        )
        key_pool = jnp.einsum(
            "tsp,tskd->pkd",
            select_f,
            key_part.reshape(tile_count, slot_count, tile_size, HEAD),
            precision=lax.Precision.HIGHEST,
        )
        value_pool = jnp.einsum(
            "tsp,tskd->pkd",
            select_f,
            value_part.reshape(tile_count, slot_count, tile_size, HEAD),
            precision=lax.Precision.HIGHEST,
        )
        return (query_out, attended, key_pool, value_pool)

    heads_first = (
        jnp.moveaxis(query_tiles.reshape(tile_count, tile_size, head_count, HEAD), 2, 0),
        jnp.moveaxis(dout_tiles.reshape(tile_count, tile_size, head_count, HEAD), 2, 0),
        jnp.moveaxis(window_key, 2, 0),
        jnp.moveaxis(window_value, 2, 0),
    )
    query_out, attended, key_pool, value_pool = lax.map(per_head, heads_first)
    query_out = jnp.moveaxis(query_out, 0, 2).reshape(tile_count, tile_size, features)
    attended = jnp.moveaxis(attended, 0, 2).reshape(tile_count, tile_size, features)
    key_pool = jnp.moveaxis(key_pool, 0, 2).reshape(pool_count, tile_size, features)
    value_pool = jnp.moveaxis(value_pool, 0, 2).reshape(pool_count, tile_size, features)
    return (query_out, attended, key_pool, value_pool)


def weight_terms(rows_in, attended_flat):
    return lax.dot_general(
        rows_in, attended_flat, (((0,), (0,)), ((), ())), preferred_element_type=jnp.float32
    )


def shards(queries, key_states, value_states, out_grad, out_weight, win_time, win_space, tile_len):
    tokens_here = queries.shape[1]
    features = queries.shape[2]
    tile_count = tokens_here // TILE
    slab_count = lax.axis_size("tm")
    slab_index = lax.axis_index("tm")
    preceding = passed_along((key_states, value_states), "tm", 1)
    following = passed_along((key_states, value_states), "tm", -1)
    pool_key = jnp.concatenate((preceding[0][0], key_states[0], following[0][0]), axis=0).reshape(
        3 * tile_count, TILE, features
    )
    pool_value = jnp.concatenate(
        (preceding[1][0], value_states[0], following[1][0]), axis=0
    ).reshape(3 * tile_count, TILE, features)
    all_len = tile_len[0]
    pool_len = jnp.concatenate(
        [
            lax.dynamic_slice_in_dim(
                all_len, (slab_index + offset + slab_count) % slab_count * tile_count, tile_count
            )
            for offset in (-1, 0, 1)
        ]
    )
    centre = tile_count + lax.broadcasted_iota(jnp.int32, (tile_count, 1), 0)
    slot_codes = jnp.concatenate((centre, (win_time[0] + 1) * tile_count + win_space[0]), axis=1)
    rows_in = out_grad[0]
    head_grad = jnp.dot(
        rows_in,
        lax.all_gather(out_weight, "dp", axis=0, tiled=True),
        preferred_element_type=jnp.float32,
    ).astype(jnp.bfloat16)
    query_out, attended, key_pool, value_pool = slab_grads(
        queries[0].reshape(tile_count, TILE, features),
        head_grad.reshape(tile_count, TILE, features),
        pool_key,
        pool_value,
        pool_len,
        slot_codes,
    )
    to_prev = (
        key_pool[:tile_count].astype(jnp.bfloat16),
        value_pool[:tile_count].astype(jnp.bfloat16),
    )
    to_next = (
        key_pool[2 * tile_count :].astype(jnp.bfloat16),
        value_pool[2 * tile_count :].astype(jnp.bfloat16),
    )
    from_next = passed_along((to_prev[0], to_prev[1]), "tm", -1)
    from_prev = passed_along((to_next[0], to_next[1]), "tm", 1)
    key_grad = (
        key_pool[tile_count : 2 * tile_count]
        + from_next[0].astype(jnp.float32)
        + from_prev[0].astype(jnp.float32)
    )
    value_grad = (
        value_pool[tile_count : 2 * tile_count]
        + from_next[1].astype(jnp.float32)
        + from_prev[1].astype(jnp.float32)
    )
    attended_flat = attended.reshape(tokens_here, features)
    weight_grad = lax.psum_scatter(
        weight_terms(rows_in, attended_flat), ("tm", "dp"), scatter_dimension=0, tiled=True
    )
    full_shape = (1, tokens_here, features)
    return (
        query_out.reshape(full_shape),
        key_grad.astype(jnp.bfloat16).reshape(full_shape),
        value_grad.astype(jnp.bfloat16).reshape(full_shape),
        weight_grad,
    )


def solution(mesh):
    in_specs = (
        P("dp", "tm", None),
        P("dp", "tm", None),
        P("dp", "tm", None),
        P("dp", "tm", None),
        P("dp", None),
        P("dp", "tm", None),
        P("dp", "tm", None),
        P("dp", None),
    )
    out_specs = (
        P("dp", "tm", None),
        P("dp", "tm", None),
        P("dp", "tm", None),
        P(("tm", "dp"), None),
    )
    return jax.shard_map(shards, mesh=mesh, in_specs=in_specs, out_specs=out_specs, check_vma=False)
```

profile of v0, /device:TPU:0, one launch (start us, length us, event | category | flops | bytes accessed | tf_op | source)
XLA Modules:
  0.0 1141.1 jit_solution(2620342673865555790)
XLA Ops:
  13.0 5.4 collective-permute-start.1
  22.7 5.8 reshape_reshape_squeeze.3
  29.7 79.6 %collective-permute-done.3 = bf16[1,768,1536]{2,1,0:T(8,128)(2,1)} collective-permute-done((bf16[1,768,1536]{2,1,0:T(8,128)(2,1)}, bf16[1,768,1536]{2,1,0:T(8,128)(2,1)}, u32[]{:S(2)}, u32[]{:S(2)}) %collective-permute-start.3) | collective-permute-done | bytes 2359328 | tf_op jit(solution)/shard_map/ppermute | solution.py:14
  114.6 6.5 pad_maximum_fusion.1
  121.1 8.2 gather_fusion.1
  129.3 28.1 %collective-permute-done.1 = bf16[1,768,1536]{2,1,0:T(8,128)(2,1)} collective-permute-done((bf16[1,768,1536]{2,1,0:T(8,128)(2,1)}, bf16[1,768,1536]{2,1,0:T(8,128)(2,1)}, u32[]{:S(2)}, u32[]{:S(2)}) %collective-permute-start.1) | collective-permute-done | bytes 2359328 | tf_op jit(solution)/shard_map/ppermute | solution.py:14
  160.8 6.4 pad_maximum_fusion
  167.2 8.2 gather_fusion
  175.4 14.4 %broadcast_select_fusion = (bf16[8,384,1536]{2,1,0:T(8,128)(2,1)}, bf16[8,384,1536]{2,1,0:T(8,128)(2,1)}) fusion(bf16[8,384,1536]{2,1,0:T(8,128)(2,1)} %gather_fusion.1, pred[8]{0:T(512)(128)(4,1)S(1)} %compare_and_fusion, bf16[8,384,1536]{2,1,0:T(8,128)(2,1)} %gather_fusion), kind=kLoop, calls=%fused_computation.55 | loop fusion | flops 9437184 | bytes 37748744 | tf_op jit(solution)/shard_map/jit(_take)/select_n | solution.py:36
  189.9 12.8 %copy.80 = bf16[8,384,1536]{1,0,2:T(8,128)(2,1)} copy(bf16[8,384,1536]{2,1,0:T(8,128)(2,1)} %get-tuple-element.203) | data formatting | bytes 18874368 | tf_op jit(solution)/shard_map/jit(_take)/select_n | solution.py:33
  202.6 18.3 %reshape.111 = bf16[2,1536,12,128]{1,0,3,2:T(2,128)(2,1)} reshape(bf16[8,384,1536]{1,0,2:T(8,128)(2,1)} %copy.80) | data formatting | bytes 18874368 | tf_op jit(solution)/shard_map/reshape | solution.py:33
  221.0 12.8 %copy.82 = bf16[8,384,1536]{1,0,2:T(8,128)(2,1)} copy(bf16[8,384,1536]{2,1,0:T(8,128)(2,1)} %get-tuple-element.202) | data formatting | bytes 18874368 | tf_op jit(solution)/shard_map/jit(_take)/select_n | solution.py:36
  233.8 18.3 %reshape.113 = bf16[2,1536,12,128]{1,0,3,2:T(2,128)(2,1)} reshape(bf16[8,384,1536]{1,0,2:T(8,128)(2,1)} %copy.82) | data formatting | bytes 18874368 | tf_op jit(solution)/shard_map/reshape | solution.py:36
  252.1 7.4 convolution_convert_fusion.1
  263.7 5.8 reshape_reshape.9
  269.5 589.4 %while.17 = (s32[]{:T(128)}, bf16[12,2,384,128]{3,2,1,0:T(8,128)(2,1)}, bf16[12,2,384,128]{3,2,1,0:T(8,128)(2,1)}, f32[12,6,384,128]{2,3,0,1:T(8,128)}, f32[12,6...) while((s32[]{:T(128)}, ...), condition=%wide.region_5.7_spmd.clone, body=%wide.region_1.0_spmd.clone.sunk | while | flops 1881444352 | bytes 85405072 | solution.py:94
  858.9 6.8 copy.92
  867.8 6.4 convolution_bitcast_fusion
  874.3 10.5 bitcast_convert_fusion
  906.1 5.5 reshape.143
  919.5 36.1 %collective-permute-done.5 = bf16[2,384,1536]{1,2,0:T(8,128)(2,1)} collective-permute-done((bf16[2,384,1536]{1,2,0:T(8,128)(2,1)}, bf16[2,384,1536]{1,2,0:T(8,128)(2,1)}, u32[]{:S(2)}, u32[]{:S(2)}) %collective-permute-start.5) | collective-permute-done | bytes 2359328 | tf_op jit(solution)/shard_map/ppermute | solution.py:14
  964.8 41.3 %collective-permute-done.7 = bf16[2,384,1536]{1,2,0:T(8,128)(2,1)} collective-permute-done((bf16[2,384,1536]{1,2,0:T(8,128)(2,1)}, bf16[2,384,1536]{1,2,0:T(8,128)(2,1)}, u32[]{:S(2)}, u32[]{:S(2)}) %collective-permute-start.7) | collective-permute-done | bytes 2359328 | tf_op jit(solution)/shard_map/ppermute | solution.py:14
  1006.2 5.8 fusion.52
  1016.3 115.4 %all-reduce.3.cloned.1.call-done = f32[1536,1536]{0,1:T(8,128)} async-done(((f32[1536,1536]{0,1:T(8,128)}), f32[1536,1536]{0,1:T(8,128)}) %all-reduce.3.cloned.1.call-update) | async-done | bytes 9437200
  (473 shorter events, 659.8 us)
Async XLA Ops:
  7.2 244.9 %copy-start = (bf16[1,768,1536]{2,1,0:T(8,128)(2,1)S(1)}, bf16[1,768,1536]{2,1,0:T(8,128)(2,1)}, u32[]{:S(2)}) copy-start(bf16[1,768,1536]{2,1,0:T(8,128)(2,1)} %param.15) | copy-start | bytes 7077892
  7.2 244.9 %all-gather.2.cloned.1.call-start = ((), (), s32[]{:S(2)}) async-start(), calls=%async_computation | async-start | bytes 5308416 | tf_op jit(solution)/shard_map/all_gather | solution.py:136
  7.9 1123.8 %all-reduce.3.cloned.1.call-start = ((), (), s32[]{:S(2)}) async-start(), calls=%async_computation.1 | async-start | bytes 18874368
  8.0 101.3 %collective-permute-start.3 = (bf16[1,768,1536]{2,1,0:T(8,128)(2,1)}, bf16[1,768,1536]{2,1,0:T(8,128)(2,1)}, u32[]{:S(2)}, u32[]{:S(2)}) collective-permute-start(bf16[1,768,1536]{2,1,0:T(8,128)(2,1)} %param.14), channel_id=1, source_target_pairs={{0,120},{8,0},{16,8},{24,16},{32,24},{40,32},{48,40},{56,48},{64,5... | collective-permute-start | bytes 7077896 | tf_op jit(solution)/shard_map/ppermute | solution.py:14
  13.0 101.6 %collective-permute-start.2 = (bf16[1,768,1536]{2,1,0:T(8,128)(2,1)}, bf16[1,768,1536]{2,1,0:T(8,128)(2,1)}, u32[]{:S(2)}, u32[]{:S(2)}) collective-permute-start(bf16[1,768,1536]{2,1,0:T(8,128)(2,1)} %param.14), channel_id=1, source_target_pairs={{0,8},{8,16},{16,24},{24,32},{32,40},{40,48},{48,56},{56,64},{64,7... | collective-permute-start | bytes 7077896 | tf_op jit(solution)/shard_map/ppermute | solution.py:14
  13.0 144.4 %collective-permute-start.1 = (bf16[1,768,1536]{2,1,0:T(8,128)(2,1)}, bf16[1,768,1536]{2,1,0:T(8,128)(2,1)}, u32[]{:S(2)}, u32[]{:S(2)}) collective-permute-start(bf16[1,768,1536]{2,1,0:T(8,128)(2,1)} %param.13), channel_id=1, source_target_pairs={{0,120},{8,0},{16,8},{24,16},{32,24},{40,32},{48,40},{56,48},{64,5... | collective-permute-start | bytes 7077896 | tf_op jit(solution)/shard_map/ppermute | solution.py:14
  18.4 142.4 %collective-permute-start = (bf16[1,768,1536]{2,1,0:T(8,128)(2,1)}, bf16[1,768,1536]{2,1,0:T(8,128)(2,1)}, u32[]{:S(2)}, u32[]{:S(2)}) collective-permute-start(bf16[1,768,1536]{2,1,0:T(8,128)(2,1)} %param.13), channel_id=1, source_target_pairs={{0,8},{8,16},{16,24},{24,32},{32,40},{40,48},{48,56},{56,64},{64,7... | collective-permute-start | bytes 7077896 | tf_op jit(solution)/shard_map/ppermute | solution.py:14
  22.7 5.8 copy-start.7
  22.7 5.8 copy-start.8
  22.7 6.0 copy-start.6
  287.8 5.7 copy-start.5
  336.9 5.7 copy-start.5
  386.0 5.7 copy-start.5
  435.2 5.7 copy-start.5
  484.3 5.7 copy-start.5
  582.6 5.7 copy-start.5
  631.8 5.7 copy-start.5
  680.9 5.7 copy-start.5
  779.0 5.7 copy-start.5
  828.1 5.7 copy-start.5
  887.6 68.0 %collective-permute-start.5 = (bf16[2,384,1536]{1,2,0:T(8,128)(2,1)}, bf16[2,384,1536]{1,2,0:T(8,128)(2,1)}, u32[]{:S(2)}, u32[]{:S(2)}) collective-permute-start(bf16[2,384,1536]{1,2,0:T(8,128)(2,1)} %bitcast.21), channel_id=1, source_target_pairs={{0,8},{8,16},{16,24},{24,32},{32,40},{40,48},{48,56},{56,64},{64,7... | collective-permute-start | bytes 7077896 | tf_op jit(solution)/shard_map/ppermute | solution.py:14
  887.6 68.0 %collective-permute-start.4 = (bf16[2,384,1536]{1,2,0:T(8,128)(2,1)}, bf16[2,384,1536]{1,2,0:T(8,128)(2,1)}, u32[]{:S(2)}, u32[]{:S(2)}) collective-permute-start(bf16[2,384,1536]{1,2,0:T(8,128)(2,1)} %bitcast.20), channel_id=1, source_target_pairs={{0,120},{8,0},{16,8},{24,16},{32,24},{40,32},{48,40},{56,48},{64,5... | collective-permute-start | bytes 7077896 | tf_op jit(solution)/shard_map/ppermute | solution.py:14
  895.8 110.4 %collective-permute-start.7 = (bf16[2,384,1536]{1,2,0:T(8,128)(2,1)}, bf16[2,384,1536]{1,2,0:T(8,128)(2,1)}, u32[]{:S(2)}, u32[]{:S(2)}) collective-permute-start(bf16[2,384,1536]{1,2,0:T(8,128)(2,1)} %bitcast.26), channel_id=1, source_target_pairs={{0,8},{8,16},{16,24},{24,32},{32,40},{40,48},{48,56},{56,64},{64,7... | collective-permute-start | bytes 7077896 | tf_op jit(solution)/shard_map/ppermute | solution.py:14
  895.8 110.4 %collective-permute-start.6 = (bf16[2,384,1536]{1,2,0:T(8,128)(2,1)}, bf16[2,384,1536]{1,2,0:T(8,128)(2,1)}, u32[]{:S(2)}, u32[]{:S(2)}) collective-permute-start(bf16[2,384,1536]{1,2,0:T(8,128)(2,1)} %bitcast.25), channel_id=1, source_target_pairs={{0,120},{8,0},{16,8},{24,16},{32,24},{40,32},{48,40},{56,48},{64,5... | collective-permute-start | bytes 7077896 | tf_op jit(solution)/shard_map/ppermute | solution.py:14
  (50 other events, 165.7 us)
Sparse Core Ops, SparseCore 0:
  9.7 104.5 all-gather.1
  874.4 257.2 all-reduce.2
where the time goes:
time: 1150 us; the launch traced here: 1140 us
  local copies, waits for them, and re-layouts  391 us (34%)
  waiting for transfers between devices  310 us (27%)
  matrix products  299 us (26%)
  other arithmetic  105 us (9%)
  starting transfers between devices  21.2 us (2%)
  between operations  14.1 us (1%)
    ppermute x8, waiting for transfers between devices, passed_along(): lax.ppermute(array, axis, [(i, (i + by) % size) for i in range(size)])  194 us
    dynamic_slice x96, local copies, waits for them, and re-layouts, slab_grads(): query_out, attended, key_pool, value_pool = lax.map(per_head, heads_first)  135 us
    unnamed x3, waiting for transfers between devices  116 us
    dynamic_update_slice x48, local copies, waits for them, and re-layouts, slab_grads(): query_out, attended, key_pool, value_pool = lax.map(per_head, heads_first)  97.9 us
    sub x12, matrix products, per_head(): exponent = jnp.exp(scores - row_max)  57.4 us
    convert_element_type x12, other arithmetic, per_head(): weights = probs_f.astype(jnp.bfloat16)  52.6 us
    dot_general x12, matrix products, per_head(): jnp.einsum('tsp,tskd->pkd', select_f, key_part.reshape(tile_count, slot_c...  47.5 us
    dot_general x12, matrix products, per_head(): jnp.einsum('tsp,tskd->pkd', select_f, value_part.reshape(tile_count, slot...  47.3 us
  transfers between devices with their start and end apart: 10, of which 7 were waited for; matrix products, arithmetic and copies ran while one was open for 15% of the time, Pallas kernels for 0%

commit v1 on v0

v1 whole, which is shorter than its diff:
```python
import functools
import math

import jax
import jax.numpy as jnp
from jax import lax
from jax.experimental import pallas as pl
from jax.experimental.pallas import tpu as pltpu
from jax.sharding import PartitionSpec as P

HEAD = 128
TILE = 384
SLOTS = 4
TILES = 2
ROWS = TILES * TILE
HEADS = 12
FEATURES = HEADS * HEAD
POOL = 3 * TILES
SCALING = 1.0 / math.sqrt(HEAD)
LOG2E = math.log2(math.e)
GROUPS = (2, 4, 6)
CALLS = ((0, 0, 2, 0), (1, 0, 4, 0), (2, 0, 4, 1), (2, 4, 2, 2))
VMEM = 48 * 1024 * 1024
F32 = jnp.float32
BF16 = jnp.bfloat16


def nt(a, b):
    return lax.dot_general(a, b, (((1,), (1,)), ((), ())), preferred_element_type=F32)


def nn(a, b):
    return jnp.dot(a, b, preferred_element_type=F32)


def inner_swap(a):
    return lax.ppermute(a, "tm", [(i, i ^ 1) for i in range(16)])


def outer_swap(a):
    return lax.ppermute(
        a, "tm", [(i, (i + 1) % 16 if i % 2 else (i - 1) % 16) for i in range(16)]
    )


def z_shift(a, by):
    return lax.ppermute(a, "dp", [(i, (i // 4) * 4 + (i + by) % 4) for i in range(8)])


def x_low_swap(a):
    return lax.ppermute(a, "dp", [(i, (i + 4) % 8) for i in range(8)])


def y_shift(a, by):
    return lax.ppermute(a, "tm", [(i, (i + 4 * by) % 16) for i in range(16)])


def x_flip(a, flip_high, flip_low):
    pairs = []
    for tm in range(16):
        for dp in range(8):
            to_tm = tm ^ 2 if flip_high else tm
            to_dp = dp ^ 4 if flip_low else dp
            pairs.append((tm * 8 + dp, to_tm * 8 + to_dp))
    return lax.ppermute(a, ("tm", "dp"), pairs)


def project_kernel(place_ref, rows_ref, *refs):
    pieces, out_ref, held, sems = refs[:8], refs[8], refs[9], refs[10]
    z, core = place_ref[0], place_ref[1]
    copies = []
    for index, piece in enumerate(pieces):
        half = core if index < 4 else 1 - core
        source = lax.rem(z - index % 4 + 4, 4)
        for low in range(2):
            row = pl.multiple_of(low * 768 + source * 192 + half * 96, 96)
            copies.append(
                pltpu.make_async_copy(
                    piece.at[low], held.at[pl.ds(row, 96), :], sems.at[index, low]
                )
            )
    for copy in copies:
        copy.start()
    for copy in copies:
        copy.wait()

    @pl.loop(0, FEATURES // 256)
    def _(j):
        cols = pl.ds(pl.multiple_of(j * 256, 256), 256)
        out_ref[:, cols] = nn(rows_ref[...], held[:, cols]).astype(BF16)


def project(place, rows_in, pieces):
    return pl.pallas_call(
        project_kernel,
        out_shape=jax.ShapeDtypeStruct((ROWS, FEATURES), BF16),
        in_specs=[
            pl.BlockSpec(memory_space=pltpu.SMEM),
            pl.BlockSpec(memory_space=pltpu.VMEM),
        ]
        + [pl.BlockSpec(memory_space=pl.ANY)] * 8,
        out_specs=pl.BlockSpec(memory_space=pltpu.VMEM),
        scratch_shapes=[
            pltpu.VMEM((FEATURES, FEATURES), BF16),
            pltpu.SemaphoreType.DMA((8, 2)),
        ],
        compiler_params=pltpu.CompilerParams(vmem_limit_bytes=VMEM),
        cost_estimate=pl.CostEstimate(
            flops=ROWS * FEATURES, bytes_accessed=1_000_000, transcendentals=0
        ),
        name="project",
    )(place, rows_in, *pieces)


def attention_kernel(
    codes_ref, lens_ref, q_ref, g_ref, ko, vo, ki, vi, kvx, *refs
):
    dq_ref, att_ref, own_ref, in_ref, out_ref = refs[-11:-6]
    kp, vp, kt, vt, acck, accv = refs[-6:]
    for tile in range(TILES):
        part = slice(tile * TILE, (tile + 1) * TILE)
        for base, k, v in (
            (0, ko[part, :], vo[part, :]),
            (2, ki[part, :], vi[part, :]),
            (4, kvx[0, part, :], kvx[1, part, :]),
        ):
            kp[base + tile] = k
            vp[base + tile] = v
            kt[base + tile] = k.T
            vt[base + tile] = v.T
    acck[...] = jnp.zeros_like(acck)
    accv[...] = jnp.zeros_like(accv)
    place = lax.broadcasted_iota(jnp.int32, (TILE, TILE), 0)

    @pl.loop(0, TILES)
    def _(tile):
        rows = pl.ds(pl.multiple_of(tile * TILE, TILE), TILE)
        q = q_ref[rows, :]
        g = g_ref[rows, :]
        codes = [codes_ref[tile, slot] for slot in range(SLOTS)]
        scores = []
        for slot in range(SLOTS):
            s = nt(kp[codes[slot]], q) * (SCALING * LOG2E)
            scores.append(jnp.where(place < lens_ref[tile, slot], s, -jnp.inf))
        top = functools.reduce(
            jnp.maximum, [jnp.max(s, axis=0, keepdims=True) for s in scores]
        )
        powers = [jnp.exp2(s - top) for s in scores]
        total = sum(jnp.sum(e, axis=0, keepdims=True) for e in powers)
        inverse = 1.0 / total
        probs = [e * inverse for e in powers]
        weights = [p.astype(BF16) for p in probs]
        att = sum(nn(vt[codes[slot]], weights[slot]) for slot in range(SLOTS)).astype(BF16)
        att_ref[rows, :] = att.T
        rowdot = jnp.sum(g.T.astype(F32) * att.astype(F32), axis=0, keepdims=True)
        dq = jnp.zeros((HEAD, TILE), F32)
        for slot in range(SLOTS):
            code = codes[slot]
            prob_grad = nt(vp[code], g)
            dscore = (probs[slot] * (prob_grad - rowdot)).astype(BF16)
            dq += nn(kt[code], dscore)
            acck[code] += nn(dscore, q)
            accv[code] += nn(weights[slot], g)
        dq_ref[rows, :] = (dq * SCALING).astype(BF16).T

    for tile in range(TILES):
        part = slice(tile * TILE, (tile + 1) * TILE)
        for base, ref in ((0, own_ref), (2, in_ref), (4, out_ref)):
            ref[0, part, :] = (acck[base + tile] * SCALING).astype(ref.dtype)
            ref[1, part, :] = accv[base + tile].astype(ref.dtype)


def attention(codes, lens, q, g, ko, vo, ki, vi, kvx, first, skip, heads, inside, held, width):
    at_head = pl.BlockSpec((ROWS, HEAD), lambda i: (0, first + i))
    pair = pl.BlockSpec((2, ROWS, HEAD), lambda i: (0, 0, skip + i))
    part = pl.BlockSpec((2, ROWS, HEAD), lambda i: (0, 0, inside + i))
    smem = pl.BlockSpec(memory_space=pltpu.SMEM)
    operands = [codes, lens, q, g, ko, vo, ki, vi, kvx]
    in_specs = [smem, smem] + [at_head] * 6 + [pair]
    aliases = {}
    for index, array in enumerate(held):
        if array is not None:
            aliases[len(operands)] = index
            operands.append(array)
            in_specs.append(pl.BlockSpec(memory_space=pl.ANY))
    whole = jax.ShapeDtypeStruct((ROWS, FEATURES), BF16)
    macs = 6 * heads * TILES * TILE * SLOTS * TILE * HEAD
    return pl.pallas_call(
        attention_kernel,
        grid=(heads,),
        out_shape=[
            whole,
            whole,
            jax.ShapeDtypeStruct((2, ROWS, width), F32),
            jax.ShapeDtypeStruct((2, ROWS, width), BF16),
            jax.ShapeDtypeStruct((2, ROWS, width), BF16),
        ],
        in_specs=in_specs,
        out_specs=[at_head, at_head, part, part, part],
        scratch_shapes=[
            pltpu.VMEM((POOL, TILE, HEAD), BF16),
            pltpu.VMEM((POOL, TILE, HEAD), BF16),
            pltpu.VMEM((POOL, HEAD, TILE), BF16),
            pltpu.VMEM((POOL, HEAD, TILE), BF16),
            pltpu.VMEM((POOL, TILE, HEAD), F32),
            pltpu.VMEM((POOL, TILE, HEAD), F32),
        ],
        input_output_aliases=aliases,
        compiler_params=pltpu.CompilerParams(vmem_limit_bytes=VMEM),
        cost_estimate=pl.CostEstimate(
            flops=macs // 64, bytes_accessed=ROWS * width, transcendentals=0
        ),
        name="attention",
    )(*operands)


def finish_kernel(own_ref, in_ref, out_ref, *refs):
    for index, ref in enumerate(refs[-2:]):
        total = own_ref[index] + in_ref[index].astype(F32) + out_ref[index].astype(F32)
        ref[...] = total.astype(BF16)


def finish(own, from_in, from_out, first, held):
    width = own.shape[2]
    step = 256
    pair = pl.BlockSpec((2, ROWS, step), lambda i: (0, 0, i))
    place = pl.BlockSpec((ROWS, step), lambda i: (0, first * HEAD // step + i))
    whole = jax.ShapeDtypeStruct((ROWS, FEATURES), BF16)
    operands = [own, from_in, from_out] + list(held)
    return pl.pallas_call(
        finish_kernel,
        grid=(width // step,),
        out_shape=[whole, whole],
        in_specs=[pair] * 3 + [pl.BlockSpec(memory_space=pl.ANY)] * len(held),
        out_specs=[place, place],
        input_output_aliases={3 + i: i for i in range(len(held))},
        compiler_params=pltpu.CompilerParams(vmem_limit_bytes=VMEM),
        cost_estimate=pl.CostEstimate(
            flops=ROWS * width, bytes_accessed=ROWS * width, transcendentals=0
        ),
        name="finish",
    )(*operands)


def picked(array, axis, index):
    return lax.dynamic_index_in_dim(array, index, axis, keepdims=False)


def weight_kernel(core_ref, rows_ref, att_ref, *refs):
    for base, core in ((0, core_ref[0]), (2, 1 - core_ref[0])):
        rows = rows_ref[pl.ds(pl.multiple_of(core * 96, 96), 96), :]
        for side in range(2):
            cols = slice(side * 768, (side + 1) * 768)
            ref = refs[base + side]
            ref[0] = nn(rows, att_ref[:, cols]).astype(ref.dtype)


def weight_parts(core, rows_t, att):
    block = pl.BlockSpec((1, 96, 768), lambda i: (i, 0, 0))
    return pl.pallas_call(
        weight_kernel,
        grid=(8,),
        out_shape=[
            jax.ShapeDtypeStruct((8, 96, 768), kind) for kind in (F32, F32, BF16, BF16)
        ],
        in_specs=[
            pl.BlockSpec(memory_space=pltpu.SMEM),
            pl.BlockSpec((192, ROWS), lambda i: (i, 0)),
            pl.BlockSpec((ROWS, FEATURES), lambda i: (0, 0)),
        ],
        out_specs=[block] * 4,
        compiler_params=pltpu.CompilerParams(vmem_limit_bytes=VMEM),
        cost_estimate=pl.CostEstimate(
            flops=ROWS * FEATURES, bytes_accessed=1_000_000, transcendentals=0
        ),
        name="weight_parts",
    )(core, rows_t, att)


def axis_sum(held, axis, index, shift):
    got = [shift(picked(held, axis, (index + by) % 4).astype(BF16), by) for by in (1, 2, 3)]
    return picked(held, axis, index) + sum(a.astype(F32) for a in got)


def x_sum(held, tm, dp):
    x_high, x_low = (tm // 2) % 2, dp // 4
    got = []
    for high, low in ((0, 1), (1, 0), (1, 1)):
        to_high = x_high ^ 1 if high else x_high
        to_low = x_low ^ 1 if low else x_low
        block = picked(picked(held, 0, to_high), 0, to_low)
        got.append(x_flip(block.astype(BF16), high, low))
    own = picked(picked(held, 0, x_high), 0, x_low)
    return own + sum(a.astype(F32) for a in got)


def shards(queries, key_states, value_states, out_grad, out_weight, win_time, win_space, tile_len):
    tm, dp = lax.axis_index("tm"), lax.axis_index("dp")
    core, z = tm % 2, dp % 4
    q, k, v, rows_in = queries[0], key_states[0], value_states[0], out_grad[0]

    step = jnp.concatenate((jnp.zeros((TILES, 1), jnp.int32), win_time[0]), axis=1)
    own = lax.broadcasted_iota(jnp.int32, (TILES, 1), 0)
    space = jnp.concatenate((own, win_space[0]), axis=1)
    to_inner = (step == 1) == (core == 0)
    codes = jnp.where(step == 0, 0, jnp.where(to_inner, 2, 4)) + space
    named = ((tm + step + 16) % 16) * TILES + space
    chosen = named[:, :, None] == lax.broadcasted_iota(jnp.int32, (TILES, SLOTS, 32), 2)
    lens = jnp.sum(jnp.where(chosen, tile_len[0][None, None, :], 0), axis=2)

    starts = [sum(GROUPS[:i]) for i in range(len(GROUPS))]
    together = lax.optimization_barrier

    def outgoing(i):
        cols = slice(starts[i] * HEAD, (starts[i] + GROUPS[i]) * HEAD)
        return jnp.stack((k[:, cols], v[:, cols]))

    x_low = dp // 4
    half = lax.dynamic_slice_in_dim(out_weight, core * 96, 96, 0)
    leaving = [outgoing(i) for i in range(len(GROUPS))]
    other = x_low_swap(half)
    leaving[0], other = together((leaving[0], other))
    arriving = [outer_swap(leaving[0])]
    both = jnp.stack((jnp.where(x_low == 0, half, other), jnp.where(x_low == 0, other, half)))
    mine = [both] + [z_shift(both, by) for by in (1, 2, 3)]
    leaving[1], mine[1] = together((leaving[1], mine[1]))
    arriving.append(outer_swap(leaving[1]))
    leaving[2], arriving[0] = together((leaving[2], arriving[0]))
    arriving.append(outer_swap(leaving[2]))
    ki, vi = inner_swap(k), inner_swap(v)
    ready, arriving[0] = together((tuple(mine), arriving[0]))
    theirs = [inner_swap(a) for a in ready]
    rows_t = together(together((rows_in, both))[0].T)
    place = jnp.stack((z, core)).astype(jnp.int32)
    place, arriving[1] = together((place, arriving[1]))
    head_grad = project(place, rows_in, mine + theirs)


    held = [None] * 5
    inside, first, parts, firsts = 0, 0, [], []
    for group, skip, heads, which in CALLS:
        width = sum(call[2] for call in CALLS if call[3] == which) * HEAD
        held = attention(
            codes, lens, q, head_grad, k, v, ki, vi, arriving[group],
            first, skip, heads, inside, held, width,
        )
        inside += heads
        first += heads
        if inside * HEAD == width:
            parts.append((held[2], inner_swap(held[3]), outer_swap(held[4])))
            firsts.append(first - inside)
            held = list(held[:2]) + [None] * 3
            inside = 0
    dq, att = held[:2]
    keep_a, keep_b, send_a, send_b = weight_parts(place[1:], rows_t, att)
    own, from_in, from_out = parts[0]
    send_a, send_b, from_out = together((send_a, send_b, from_out))
    parts[0] = (own, from_in, from_out)
    y = tm // 4
    late = (keep_b + inner_swap(send_b).astype(F32)).reshape(4, 2, 2, 4, 12, 768)
    early = (keep_a + inner_swap(send_a).astype(F32)).reshape(4, 2, 96, 768)
    early = axis_sum(early, 0, y, y_shift).reshape(2, 2, 4, 12, 768)
    late = axis_sum(late, 3, z, z_shift)
    own, from_in, from_out = parts[1]
    early, late, from_out = together((early, late, from_out))
    parts[1] = (own, from_in, from_out)
    early = axis_sum(early, 2, z, z_shift)
    late = axis_sum(late, 0, y, y_shift)
    own, from_in, from_out = parts[2]
    early, late, from_out = together((early, late, from_out))
    parts[2] = (own, from_in, from_out)
    weight_grad = x_sum(jnp.concatenate((early, late), axis=3), tm, dp)
    grads = ()
    for part, first in zip(parts, firsts):
        grads = finish(*part, first, grads)
    dk, dv = grads
    return dq[None], dk[None], dv[None], weight_grad


def solution(mesh):
    tokens = P("dp", "tm", None)
    in_specs = (tokens, tokens, tokens, tokens, P("dp", None), tokens, tokens, P("dp", None))
    out_specs = (tokens, tokens, tokens, P(("tm", "dp"), None))
    return jax.shard_map(shards, mesh=mesh, in_specs=in_specs, out_specs=out_specs, check_vma=False)
```

time: 1150 us -> 282 us (0.25)
  local copies, waits for them, and re-layouts: 391 us -> 25.3 us
  matrix products: 299 us -> 0 us
  waiting for transfers between devices: 310 us -> 70.6 us
  Pallas kernels: 0 us -> 120 us
  other arithmetic: 105 us -> 10 us
  starting transfers between devices: 21.2 us -> 50.1 us
  between operations: 14.1 us -> 1.56 us
    dot_general x86 -> x0, matrix products: 241 us -> none  [the longest x12 47.5 us: per_head(): jnp.einsum('tsp,tskd->pkd', select_f, key_part.reshape(tile_count, slot_c...]
    dynamic_slice x97 -> x4, local copies, waits for them, and re-layouts: 135 us -> 3.18 us  [the longest x3 2.14 us: picked(): return lax.dynamic_index_in_dim(array, index, axis, keepdims=False)]
    ppermute x8 -> x36, waiting for transfers between devices: 194 us -> 70.6 us  [the longest x9 35.8 us: z_shift(): lax.ppermute(a, 'dp', [(i, i // 4 * 4 + (i + by) % 4) for i in range(8)])]
    pallas_call x0 -> x9, Pallas kernels: none -> 120 us  [the longest x4 88.6 us: attention(): pl.pallas_call(attention_kernel, grid=(heads,), out_shape=[whole, whole,...]
    unnamed x3 -> x0, waiting for transfers between devices: 116 us -> none
    dynamic_update_slice x48 -> x0, local copies, waits for them, and re-layouts: 97.9 us -> none  [slab_grads(): query_out, attended, key_pool, value_pool = lax.map(per_head, heads_first)]
    convert_element_type x14 -> x0, other arithmetic: 63.3 us -> none  [the longest x12 52.6 us: per_head(): weights = probs_f.astype(jnp.bfloat16)]
    sub x12 -> x0, matrix products: 57.4 us -> none  [per_head(): exponent = jnp.exp(scores - row_max)]
  transfers between devices with their start and end apart: 10 -> 36, of which waited for: 7 -> 19; matrix products, arithmetic and copies ran while one was open for 15% -> 9% of each run, Pallas kernels for 0% -> 43%
where the time goes in v1:
time: 282 us; the launch traced here: 277 us
  Pallas kernels  120 us (43%)
  waiting for transfers between devices  70.6 us (25%)
  starting transfers between devices  50.1 us (18%)
  local copies, waits for them, and re-layouts  25.3 us (9%)
  other arithmetic  10 us (4%)
    pallas_call x4, Pallas kernels, attention(): pl.pallas_call(attention_kernel, grid=(heads,), out_shape=[whole, whole,...  88.6 us
    ppermute x9, waiting for transfers between devices, z_shift(): lax.ppermute(a, 'dp', [(i, i // 4 * 4 + (i + by) % 4) for i in range(8)])  35.8 us
    ppermute x6, starting transfers between devices, outer_swap(): lax.ppermute(a, 'tm', [(i, (i + 1) % 16 if i % 2 else (i - 1) % 16) for i...  23.2 us
    ppermute x9, starting transfers between devices, z_shift(): lax.ppermute(a, 'dp', [(i, i // 4 * 4 + (i + by) % 4) for i in range(8)])  15.1 us
    ppermute x6, waiting for transfers between devices, y_shift(): return lax.ppermute(a, 'tm', [(i, (i + 4 * by) % 16) for i in range(16)])  14.6 us
    unnamed x53, local copies, waits for them, and re-layouts  14.5 us
    pallas_call x1, Pallas kernels, weight_parts(): pl.pallas_call(weight_kernel, grid=(8,), out_shape=[jax.ShapeDtypeStruct(...  10.8 us
    ppermute x6, waiting for transfers between devices, outer_swap(): lax.ppermute(a, 'tm', [(i, (i + 1) % 16 if i % 2 else (i - 1) % 16) for i...  10.7 us
  transfers between devices with their start and end apart: 36, of which 19 were waited for; matrix products, arithmetic and copies ran while one was open for 9% of the time, Pallas kernels for 43%

profile of v1, /device:TPU:0, one launch (start us, length us, event | category | flops | bytes accessed | tf_op | source)
XLA Modules:
  0.0 277.5 jit_solution(13498947907034815252)
XLA Ops:
  6.2 4.2 %collective-permute-done = bf16[96,1536]{1,0:T(8,128)(2,1)S(1)} collective-permute-done((bf16[96,1536]{1,0:T(8,128)(2,1)S(1)}, bf16[96,1536]{1,0:T(8,128)(2,1)S(1)}, u32[]{:S(2)}, u32[]{:S(2)}) %collective-permute-start) | collective-permute-done | bytes 294944 | tf_op jit(solution)/shard_map/ppermute | solution.py:51
  12.8 3.8 %collective-permute-start.5 = (bf16[2,768,256]{2,1,0:T(8,128)(2,1)S(1)}, bf16[2,768,256]{2,1,0:T(8,128)(2,1)S(1)}, u32[]{:S(2)}, u32[]{:S(2)}) collective-permute-start(bf16[2,768,256]{2,1,0:T(8,128)(2,1)S(1)} %pad_maximum_fusion.2), channel_id=1, source_target_pairs={{0,120},{8,16},{16,8},{24,32},{32,24},{40,48},{48,40},{56,64},{64,... | collective-permute-start | bytes 2359304 | tf_op jit(solution)/shard_map/ppermute | solution.py:41
  16.8 10.5 %collective-permute-done.1.refs_1_ = bf16[2,96,1536]{2,1,0:T(8,128)(2,1)S(1)} collective-permute-done((bf16[2,96,1536]{2,1,0:T(8,128)(2,1)S(1)}, bf16[2,96,1536]{2,1,0:T(8,128)(2,1)S(1)}, u32[]{:S(2)}, u32[]{:S(2)}) %collective-permute-start.1) | collective-permute-done | bytes 589856 | tf_op jit(solution)/shard_map/ppermute | solution.py:47
  27.4 3.4 %collective-permute-start.2 = (bf16[2,768,512]{2,1,0:T(8,128)(2,1)S(1)}, bf16[2,768,512]{2,1,0:T(8,128)(2,1)S(1)}, u32[]{:S(2)}, u32[]{:S(2)}) collective-permute-start(bf16[2,768,512]{2,1,0:T(8,128)(2,1)S(1)} %pad_maximum_fusion.1), channel_id=1, source_target_pairs={{0,120},{8,16},{16,8},{24,32},{32,24},{40,48},{48,40},{56,64},{64,... | collective-permute-start | bytes 4718600 | tf_op jit(solution)/shard_map/ppermute | solution.py:41
  32.1 3.8 %collective-permute-done.5.kvx = bf16[2,768,256]{2,1,0:T(8,128)(2,1)S(1)} collective-permute-done((bf16[2,768,256]{2,1,0:T(8,128)(2,1)S(1)}, bf16[2,768,256]{2,1,0:T(8,128)(2,1)S(1)}, u32[]{:S(2)}, u32[]{:S(2)}) %collective-permute-start.5) | collective-permute-done | bytes 786464 | tf_op jit(solution)/shard_map/ppermute | solution.py:41
  39.9 7.3 %collective-permute-done.3.refs_2_ = bf16[2,96,1536]{2,1,0:T(8,128)(2,1)S(1)} collective-permute-done((bf16[2,96,1536]{2,1,0:T(8,128)(2,1)S(1)}, bf16[2,96,1536]{2,1,0:T(8,128)(2,1)S(1)}, u32[]{:S(2)}, u32[]{:S(2)}) %collective-permute-start.3) | collective-permute-done | bytes 589856 | tf_op jit(solution)/shard_map/ppermute | solution.py:47
  47.2 11.8 %collective-permute-done.4.refs_3_ = bf16[2,96,1536]{2,1,0:T(8,128)(2,1)S(1)} collective-permute-done((bf16[2,96,1536]{2,1,0:T(8,128)(2,1)S(1)}, bf16[2,96,1536]{2,1,0:T(8,128)(2,1)S(1)}, u32[]{:S(2)}, u32[]{:S(2)}) %collective-permute-start.4) | collective-permute-done | bytes 589856 | tf_op jit(solution)/shard_map/ppermute | solution.py:47
  62.8 6.9 %collective-permute-done.2.kvx = bf16[2,768,512]{2,1,0:T(8,128)(2,1)S(1)} collective-permute-done((bf16[2,768,512]{2,1,0:T(8,128)(2,1)S(1)}, bf16[2,768,512]{2,1,0:T(8,128)(2,1)S(1)}, u32[]{:S(2)}, u32[]{:S(2)}) %collective-permute-start.2) | collective-permute-done | bytes 1572896 | tf_op jit(solution)/shard_map/ppermute | solution.py:41
  71.2 3.1 %collective-permute-start.12 = (bf16[2,768,768]{2,1,0:T(8,128)(2,1)}, bf16[2,768,768]{2,1,0:T(8,128)(2,1)}, u32[]{:S(2)}, u32[]{:S(2)}) collective-permute-start(bf16[2,768,768]{2,1,0:T(8,128)(2,1)} %pad_maximum_fusion), channel_id=1, source_target_pairs={{0,120},{8,16},{16,8},{24,32},{32,24},{40,48},{48,40},{56,64},{64,... | collective-permute-start | bytes 7077896 | tf_op jit(solution)/shard_map/ppermute | solution.py:41
  75.3 9.9 %project.1.g_ref = bf16[768,1536]{1,0:T(8,128)(2,1)} custom-call(s32[2]{0:T(128)S(1)} %pad_add_fusion.1.place_ref, bf16[768,1536]{1,0:T(8,128)(2,1)} %bitcast.105, bf16[2,96,1536]{2,1,0:T(8,128)(2,1)S(1)} %pad_maximum_fusion.3.refs_0_, bf16[2,96,1536]{2,1,0:T(8,128)(2,1)S(1)} %collective-permute-done.1.refs_1_, ...), custom_call_target="tpu_custom_call" | custom-call | flops 1179648 | bytes 1000000 | tf_op jit(solution)/shard_map/project/pallas_call | solution.py:94
  85.3 15.6 %attention.4 = (bf16[768,1536]{1,0:T(8,128)(2,1)}, bf16[768,1536]{1,0:T(8,128)(2,1)S(1)}, f32[2,768,768]{2,1,0:T(8,128)}, bf16[2,768,768]{2,1,0:T(8,128)(2,1)S(1)}, bf16[2,768,768]{2,1,0:T(8,128)(2,1)}) custom-call(s32[2,4]{1,0:T(2,128)S(1)} %get-tuple-element.127.codes_ref, s32[2,4]{1,0:T(2,128)S(1)} %select_reduce_fusion.lens_ref, ...), custom_call_target="tpu_custom_call" | custom-call | flops 28311552 | bytes 589824 | tf_op jit(solution)/shard_map/attention/pallas_call | solution.py:188
  102.5 28.7 %attention.5 = (bf16[768,1536]{1,0:T(8,128)(2,1)}, bf16[768,1536]{1,0:T(8,128)(2,1)S(1)}, f32[2,768,768]{2,1,0:T(8,128)}, bf16[2,768,768]{2,1,0:T(8,128)(2,1)}, bf16[2,768,768]{2,1,0:T(8,128)(2,1)}) custom-call(s32[2,4]{1,0:T(2,128)S(1)} %get-tuple-element.127.codes_ref, ...), custom_call_target="tpu_custom_call", output_to_operand_aliasing={{0}: (9, {}), {1}: (10, {}), {2}: (11, {}), {3}: (12, {}), ... | custom-call | flops 56623104 | bytes 589824 | tf_op jit(solution)/shard_map/attention/pallas_call | solution.py:188
  134.0 4.3 %copy.85 = bf16[1,768,1536]{1,2,0:T(8,128)(2,1)} copy(bf16[1,768,1536]{2,1,0:T(8,128)(2,1)} %param.11) | data formatting | bytes 4718592 | tf_op args[3]
  138.9 28.9 %attention.6 = (bf16[768,1536]{1,0:T(8,128)(2,1)}, bf16[768,1536]{1,0:T(8,128)(2,1)S(1)}, f32[2,768,512]{2,1,0:T(8,128)}, bf16[2,768,512]{2,1,0:T(8,128)(2,1)S(1)}, bf16[2,768,512]{2,1,0:T(8,128)(2,1)S(1)}) custom-call(s32[2,4]{1,0:T(2,128)S(1)} %get-tuple-element.127.codes_ref, ...), custom_call_target="tpu_custom_call", output_to_operand_aliasing={{0}: (9, {}), {1}: (10, {})} | custom-call | flops 56623104 | bytes 393216 | tf_op jit(solution)/shard_map/attention/pallas_call | solution.py:188
  169.6 15.2 %attention.7 = (bf16[768,1536]{1,0:T(8,128)(2,1)}, bf16[768,1536]{1,0:T(8,128)(2,1)S(1)}, f32[2,768,256]{2,1,0:T(8,128)S(1)}, bf16[2,768,256]{2,1,0:T(8,128)(2,1)S(1)}, bf16[2,768,256]{2,1,0:T(8,128)(2,1)S(1)}) custom-call(s32[2,4]{1,0:T(2,128)S(1)} %get-tuple-element.127.codes_ref, ...), custom_call_target="tpu_custom_call", output_to_operand_aliasing={{0}: (9, {}), {1}: (10, {})} | custom-call | flops 28311552 | bytes 196608 | tf_op jit(solution)/shard_map/attention/pallas_call | solution.py:188
  187.1 10.8 %weight_parts.1 = (f32[8,96,768]{2,1,0:T(8,128)S(1)}, f32[8,96,768]{2,1,0:T(8,128)}, bf16[8,96,768]{2,1,0:T(8,128)(2,1)S(1)}, bf16[8,96,768]{2,1,0:T(8,128)(2,1)}) custom-call(s32[1]{0:T(128)} %slice.27.core_ref, bf16[1536,768]{1,0:T(8,128)(2,1)} %bitcast.104, bf16[768,1536]{1,0:T(8,128)(2,1)} %copy-done), custom_call_target="tpu_custom_call" | custom-call | flops 1179648 | bytes 1000000 | tf_op jit(solution)/shard_map/weight_parts/pallas_call | solution.py:260
  202.8 4.3 %convert_add_fusion = (f32[8,96,768]{2,1,0:T(8,128)S(1)}, f32[8,96,768]{2,1,0:T(8,128)}) fusion(f32[8,96,768]{2,1,0:T(8,128)} %get-tuple-element.89, bf16[8,96,768]{2,1,0:T(8,128)(2,1)} %collective-permute-done.19, f32[8,96,768]{2,1,0:T(8,128)S(1)} %get-tuple-element.84, bf16[8,96,768]{2,1,0:T(8,128)(2,1)} %collective-permute-done.15), kind=kLoop, calls=%fused_computation.1 | loop fusion | flops 2359296 | bytes 11796480 | tf_op jit(solution)/shard_map/add | solution.py:360
  218.9 5.8 %finish.3 = (bf16[768,1536]{1,0:T(8,128)(2,1)}, bf16[768,1536]{1,0:T(8,128)(2,1)}) custom-call(f32[2,768,768]{2,1,0:T(8,128)} %get-tuple-element.99.own_ref, bf16[2,768,768]{2,1,0:T(8,128)(2,1)} %collective-permute-done.32.in_ref, bf16[2,768,768]{2,1,0:T(8,128)(2,1)} %collective-permute-done.14.out_ref), custom_call_target="tpu_custom_call" | custom-call | flops 589824 | bytes 589824 | tf_op jit(solution)/shard_map/finish/pallas_call | solution.py:230
  229.3 3.3 %collective-permute-done.20 = bf16[4,2,2,12,768]{4,1,3,2,0:T(2,128)(2,1)S(1)} collective-permute-done((bf16[4,2,2,12,768]{4,1,3,2,0:T(2,128)(2,1)S(1)}, bf16[4,2,2,12,768]{4,1,3,2,0:T(2,128)(2,1)S(1)}, u32[]{:S(2)}, u32[]{:S(2)}) %collective-permute-start.20) | collective-permute-done | bytes 294944 | tf_op jit(solution)/shard_map/ppermute | solution.py:47
  234.2 3.2 %collective-permute-done.18 = bf16[2,96,768]{2,0,1:T(2,128)(2,1)S(1)} collective-permute-done((bf16[2,96,768]{2,0,1:T(2,128)(2,1)S(1)}, bf16[2,96,768]{2,0,1:T(2,128)(2,1)S(1)}, u32[]{:S(2)}, u32[]{:S(2)}) %collective-permute-start.18) | collective-permute-done | bytes 294944 | tf_op jit(solution)/shard_map/ppermute | solution.py:55
  237.5 5.1 %collective-permute-done.17 = bf16[2,96,768]{2,0,1:T(2,128)(2,1)S(1)} collective-permute-done((bf16[2,96,768]{2,0,1:T(2,128)(2,1)S(1)}, bf16[2,96,768]{2,0,1:T(2,128)(2,1)S(1)}, u32[]{:S(2)}, u32[]{:S(2)}) %collective-permute-start.17) | collective-permute-done | bytes 294944 | tf_op jit(solution)/shard_map/ppermute | solution.py:55
  242.5 7.5 %collective-permute-start.30 = (bf16[2,768,256]{2,1,0:T(8,128)(2,1)S(1)}, bf16[2,768,256]{2,1,0:T(8,128)(2,1)S(1)}, u32[]{:S(2)}, u32[]{:S(2)}) collective-permute-start(bf16[2,768,256]{2,1,0:T(8,128)(2,1)S(1)} %copy-done.13), channel_id=1, source_target_pairs={{0,120},{8,16},{16,8},{24,32},{32,24},{40,48},{48,40},{56,64},{64,... | collective-permute-start | bytes 2359304 | tf_op jit(solution)/shard_map/ppermute | solution.py:41
  255.2 3.8 %finish.4 = (bf16[768,1536]{1,0:T(8,128)(2,1)}, bf16[768,1536]{1,0:T(8,128)(2,1)}) custom-call(f32[2,768,512]{2,1,0:T(8,128)} %get-tuple-element.96.own_ref, bf16[2,768,512]{2,1,0:T(8,128)(2,1)} %collective-permute-done.31.in_ref, bf16[2,768,512]{2,1,0:T(8,128)(2,1)} %collective-permute-done.23.out_ref, ...), custom_call_target="tpu_custom_call", output_to_operand_aliasing={{0}: (3, {}), {1}: (4, {})} | custom-call | flops 393216 | bytes 393216 | tf_op jit(solution)/shard_map/finish/pallas_call | solution.py:230
  263.8 3.6 %collective-permute-done.28 = bf16[2,2,12,768]{3,0,2,1:T(2,128)(2,1)S(1)} collective-permute-done((bf16[2,2,12,768]{3,0,2,1:T(2,128)(2,1)S(1)}, bf16[2,2,12,768]{3,0,2,1:T(2,128)(2,1)S(1)}, u32[]{:S(2)}, u32[]{:S(2)}) %collective-permute-start.28) | collective-permute-done | bytes 73760 | tf_op jit(solution)/shard_map/ppermute | solution.py:55
  (144 shorter events, 71.0 us)
Async XLA Ops:
  1.7 8.7 %collective-permute-start = (bf16[96,1536]{1,0:T(8,128)(2,1)S(1)}, bf16[96,1536]{1,0:T(8,128)(2,1)S(1)}, u32[]{:S(2)}, u32[]{:S(2)}) collective-permute-start(bf16[96,1536]{1,0:T(8,128)(2,1)S(1)} %constant_dynamic-slice_fusion.6), channel_id=1, source_target_pairs={{0,4},{1,5},{2,6},{3,7},{4,0},{5,1},{6,2},{7,3},{8,12},{9,13},{10,... | collective-permute-start | bytes 884744 | tf_op jit(solution)/shard_map/ppermute | solution.py:51
  3.4 81.9 %collective-permute-start.10 = (bf16[768,1536]{1,0:T(8,128)(2,1)}, bf16[768,1536]{1,0:T(8,128)(2,1)}, u32[]{:S(2)}, u32[]{:S(2)}) collective-permute-start(bf16[768,1536]{1,0:T(8,128)(2,1)} %bitcast.83), channel_id=1, source_target_pairs={{0,8},{8,0},{16,24},{24,16},{32,40},{40,32},{48,56},{56,48},{64,72... | collective-permute-start | bytes 7077896 | tf_op jit(solution)/shard_map/ppermute | solution.py:37
  3.4 81.9 %collective-permute-start.11 = (bf16[768,1536]{1,0:T(8,128)(2,1)}, bf16[768,1536]{1,0:T(8,128)(2,1)}, u32[]{:S(2)}, u32[]{:S(2)}) collective-permute-start(bf16[768,1536]{1,0:T(8,128)(2,1)} %bitcast.91), channel_id=1, source_target_pairs={{0,8},{8,0},{16,24},{24,16},{32,40},{40,32},{48,56},{56,48},{64,72... | collective-permute-start | bytes 7077896 | tf_op jit(solution)/shard_map/ppermute | solution.py:37
  10.5 16.8 %collective-permute-start.1 = (bf16[2,96,1536]{2,1,0:T(8,128)(2,1)S(1)}, bf16[2,96,1536]{2,1,0:T(8,128)(2,1)S(1)}, u32[]{:S(2)}, u32[]{:S(2)}) collective-permute-start(bf16[2,96,1536]{2,1,0:T(8,128)(2,1)S(1)} %pad_maximum_fusion.3.refs_0_), channel_id=1, source_target_pairs={{0,1},{1,2},{2,3},{3,0},{4,5},{5,6},{6,7},{7,4},{8,9},{9,10},{10,1... | collective-permute-start | bytes 1769480 | tf_op jit(solution)/shard_map/ppermute | solution.py:47
  12.8 23.1 %collective-permute-start.5 = (bf16[2,768,256]{2,1,0:T(8,128)(2,1)S(1)}, bf16[2,768,256]{2,1,0:T(8,128)(2,1)S(1)}, u32[]{:S(2)}, u32[]{:S(2)}) collective-permute-start(bf16[2,768,256]{2,1,0:T(8,128)(2,1)S(1)} %pad_maximum_fusion.2), channel_id=1, source_target_pairs={{0,120},{8,16},{16,8},{24,32},{32,24},{40,48},{48,40},{56,64},{64,... | collective-permute-start | bytes 2359304 | tf_op jit(solution)/shard_map/ppermute | solution.py:41
  27.4 42.3 %collective-permute-start.2 = (bf16[2,768,512]{2,1,0:T(8,128)(2,1)S(1)}, bf16[2,768,512]{2,1,0:T(8,128)(2,1)S(1)}, u32[]{:S(2)}, u32[]{:S(2)}) collective-permute-start(bf16[2,768,512]{2,1,0:T(8,128)(2,1)S(1)} %pad_maximum_fusion.1), channel_id=1, source_target_pairs={{0,120},{8,16},{16,8},{24,32},{32,24},{40,48},{48,40},{56,64},{64,... | collective-permute-start | bytes 4718600 | tf_op jit(solution)/shard_map/ppermute | solution.py:41
  30.8 16.5 %collective-permute-start.3 = (bf16[2,96,1536]{2,1,0:T(8,128)(2,1)S(1)}, bf16[2,96,1536]{2,1,0:T(8,128)(2,1)S(1)}, u32[]{:S(2)}, u32[]{:S(2)}) collective-permute-start(bf16[2,96,1536]{2,1,0:T(8,128)(2,1)S(1)} %pad_maximum_fusion.3.refs_0_), channel_id=1, source_target_pairs={{0,2},{1,3},{2,0},{3,1},{4,6},{5,7},{6,4},{7,5},{8,10},{9,11},{10,... | collective-permute-start | bytes 1769480 | tf_op jit(solution)/shard_map/ppermute | solution.py:47
  35.9 23.1 %collective-permute-start.4 = (bf16[2,96,1536]{2,1,0:T(8,128)(2,1)S(1)}, bf16[2,96,1536]{2,1,0:T(8,128)(2,1)S(1)}, u32[]{:S(2)}, u32[]{:S(2)}) collective-permute-start(bf16[2,96,1536]{2,1,0:T(8,128)(2,1)S(1)} %pad_maximum_fusion.3.refs_0_), channel_id=1, source_target_pairs={{0,3},{1,0},{2,1},{3,2},{4,7},{5,4},{6,5},{7,6},{8,11},{9,8},{10,9... | collective-permute-start | bytes 1769480 | tf_op jit(solution)/shard_map/ppermute | solution.py:47
  59.0 12.2 %collective-permute-start.7 = (bf16[2,96,1536]{2,1,0:T(8,128)(2,1)S(1)}, bf16[2,96,1536]{2,1,0:T(8,128)(2,1)}, u32[]{:S(2)}, u32[]{:S(2)}) collective-permute-start(bf16[2,96,1536]{2,1,0:T(8,128)(2,1)S(1)} %collective-permute-done.1.refs_1_), channel_id=1, source_target_pairs={{0,8},{8,0},{16,24},{24,16},{32,40},{40,32},{48,56},{56,48},{64,72... | collective-permute-start | bytes 1769480 | tf_op jit(solution)/shard_map/ppermute | solution.py:37
  62.6 11.7 %collective-permute-start.8 = (bf16[2,96,1536]{2,1,0:T(8,128)(2,1)S(1)}, bf16[2,96,1536]{2,1,0:T(8,128)(2,1)}, u32[]{:S(2)}, u32[]{:S(2)}) collective-permute-start(bf16[2,96,1536]{2,1,0:T(8,128)(2,1)S(1)} %collective-permute-done.3.refs_2_), channel_id=1, source_target_pairs={{0,8},{8,0},{16,24},{24,16},{32,40},{40,32},{48,56},{56,48},{64,72... | collective-permute-start | bytes 1769480 | tf_op jit(solution)/shard_map/ppermute | solution.py:37
  71.2 67.7 %collective-permute-start.12 = (bf16[2,768,768]{2,1,0:T(8,128)(2,1)}, bf16[2,768,768]{2,1,0:T(8,128)(2,1)}, u32[]{:S(2)}, u32[]{:S(2)}) collective-permute-start(bf16[2,768,768]{2,1,0:T(8,128)(2,1)} %pad_maximum_fusion), channel_id=1, source_target_pairs={{0,120},{8,16},{16,8},{24,32},{32,24},{40,48},{48,40},{56,64},{64,... | collective-permute-start | bytes 7077896 | tf_op jit(solution)/shard_map/ppermute | solution.py:41
  131.2 66.7 %collective-permute-start.14 = (bf16[2,768,768]{2,1,0:T(8,128)(2,1)}, bf16[2,768,768]{2,1,0:T(8,128)(2,1)}, u32[]{:S(2)}, u32[]{:S(2)}) collective-permute-start(bf16[2,768,768]{2,1,0:T(8,128)(2,1)} %get-tuple-element.87), channel_id=1, source_target_pairs={{0,120},{8,16},{16,8},{24,32},{32,24},{40,48},{48,40},{56,64},{64,... | collective-permute-start | bytes 7077896 | tf_op jit(solution)/shard_map/ppermute | solution.py:41
  133.8 84.0 %collective-permute-start.32 = (bf16[2,768,768]{2,1,0:T(8,128)(2,1)}, bf16[2,768,768]{2,1,0:T(8,128)(2,1)}, u32[]{:S(2)}, u32[]{:S(2)}) collective-permute-start(bf16[2,768,768]{2,1,0:T(8,128)(2,1)} %get-tuple-element.100), channel_id=1, source_target_pairs={{0,8},{8,0},{16,24},{24,16},{32,40},{40,32},{48,56},{56,48},{64,72... | collective-permute-start | bytes 7077896 | tf_op jit(solution)/shard_map/ppermute | solution.py:37
  198.6 52.3 %collective-permute-start.23 = (bf16[2,768,512]{2,1,0:T(8,128)(2,1)}, bf16[2,768,512]{2,1,0:T(8,128)(2,1)}, u32[]{:S(2)}, u32[]{:S(2)}) collective-permute-start(bf16[2,768,512]{2,1,0:T(8,128)(2,1)} %copy-done.9), channel_id=1, source_target_pairs={{0,120},{8,16},{16,8},{24,32},{32,24},{40,48},{48,40},{56,64},{64,... | collective-permute-start | bytes 4718600 | tf_op jit(solution)/shard_map/ppermute | solution.py:41
  201.4 53.3 %collective-permute-start.31 = (bf16[2,768,512]{2,1,0:T(8,128)(2,1)}, bf16[2,768,512]{2,1,0:T(8,128)(2,1)}, u32[]{:S(2)}, u32[]{:S(2)}) collective-permute-start(bf16[2,768,512]{2,1,0:T(8,128)(2,1)} %copy-done.8), channel_id=1, source_target_pairs={{0,8},{8,0},{16,24},{24,16},{32,40},{40,32},{48,56},{56,48},{64,72... | collective-permute-start | bytes 4718600 | tf_op jit(solution)/shard_map/ppermute | solution.py:37
  213.2 15.4 %collective-permute-start.22 = (bf16[4,2,2,12,768]{4,1,3,2,0:T(2,128)(2,1)S(1)}, bf16[4,2,2,12,768]{4,1,3,2,0:T(2,128)(2,1)S(1)}, u32[]{:S(2)}, u32[]{:S(2)}) collective-permute-start(bf16[4,2,2,12,768]{4,1,3,2,0:T(2,128)(2,1)S(1)} %bitcast.115), channel_id=1, source_target_pairs={{0,3},{1,0},{2,1},{3,2},{4,7},{5,4},{6,5},{7,6},{8,11},{9,8},{10,9... | collective-permute-start | bytes 884744 | tf_op jit(solution)/shard_map/ppermute | solution.py:47
  215.7 13.2 %collective-permute-start.21 = (bf16[4,2,2,12,768]{4,1,3,2,0:T(2,128)(2,1)S(1)}, bf16[4,2,2,12,768]{4,1,3,2,0:T(2,128)(2,1)S(1)}, u32[]{:S(2)}, u32[]{:S(2)}) collective-permute-start(bf16[4,2,2,12,768]{4,1,3,2,0:T(2,128)(2,1)S(1)} %bitcast.114), channel_id=1, source_target_pairs={{0,2},{1,3},{2,0},{3,1},{4,6},{5,7},{6,4},{7,5},{8,10},{9,11},{10,... | collective-permute-start | bytes 884744 | tf_op jit(solution)/shard_map/ppermute | solution.py:47
  217.8 14.8 %collective-permute-start.20 = (bf16[4,2,2,12,768]{4,1,3,2,0:T(2,128)(2,1)S(1)}, bf16[4,2,2,12,768]{4,1,3,2,0:T(2,128)(2,1)S(1)}, u32[]{:S(2)}, u32[]{:S(2)}) collective-permute-start(bf16[4,2,2,12,768]{4,1,3,2,0:T(2,128)(2,1)S(1)} %bitcast.113), channel_id=1, source_target_pairs={{0,1},{1,2},{2,3},{3,0},{4,5},{5,6},{6,7},{7,4},{8,9},{9,10},{10,1... | collective-permute-start | bytes 884744 | tf_op jit(solution)/shard_map/ppermute | solution.py:47
  228.6 8.8 %collective-permute-start.18 = (bf16[2,96,768]{2,0,1:T(2,128)(2,1)S(1)}, bf16[2,96,768]{2,0,1:T(2,128)(2,1)S(1)}, u32[]{:S(2)}, u32[]{:S(2)}) collective-permute-start(bf16[2,96,768]{2,0,1:T(2,128)(2,1)S(1)} %bitcast.118), channel_id=1, source_target_pairs={{0,96},{8,104},{16,112},{24,120},{32,0},{40,8},{48,16},{56,24},{64... | collective-permute-start | bytes 884744 | tf_op jit(solution)/shard_map/ppermute | solution.py:55
  228.9 13.6 %collective-permute-start.17 = (bf16[2,96,768]{2,0,1:T(2,128)(2,1)S(1)}, bf16[2,96,768]{2,0,1:T(2,128)(2,1)S(1)}, u32[]{:S(2)}, u32[]{:S(2)}) collective-permute-start(bf16[2,96,768]{2,0,1:T(2,128)(2,1)S(1)} %bitcast.117), channel_id=1, source_target_pairs={{0,64},{8,72},{16,80},{24,88},{32,96},{40,104},{48,112},{56,120},{... | collective-permute-start | bytes 884744 | tf_op jit(solution)/shard_map/ppermute | solution.py:55
  232.6 17.5 %collective-permute-start.16 = (bf16[2,96,768]{2,0,1:T(2,128)(2,1)S(1)}, bf16[2,96,768]{2,0,1:T(2,128)(2,1)S(1)}, u32[]{:S(2)}, u32[]{:S(2)}) collective-permute-start(bf16[2,96,768]{2,0,1:T(2,128)(2,1)S(1)} %bitcast.116), channel_id=1, source_target_pairs={{0,32},{8,40},{16,48},{24,56},{32,64},{40,72},{48,80},{56,88},{64,... | collective-permute-start | bytes 884744 | tf_op jit(solution)/shard_map/ppermute | solution.py:55
  237.5 36.0 %collective-permute-start.13 = (bf16[2,768,256]{2,1,0:T(8,128)(2,1)S(1)}, bf16[2,768,256]{2,1,0:T(8,128)(2,1)S(1)}, u32[]{:S(2)}, u32[]{:S(2)}) collective-permute-start(bf16[2,768,256]{2,1,0:T(8,128)(2,1)S(1)} %copy-done.11), channel_id=1, source_target_pairs={{0,8},{8,0},{16,24},{24,16},{32,40},{40,32},{48,56},{56,48},{64,72... | collective-permute-start | bytes 2359304 | tf_op jit(solution)/shard_map/ppermute | solution.py:37
  242.5 26.2 %collective-permute-start.30 = (bf16[2,768,256]{2,1,0:T(8,128)(2,1)S(1)}, bf16[2,768,256]{2,1,0:T(8,128)(2,1)S(1)}, u32[]{:S(2)}, u32[]{:S(2)}) collective-permute-start(bf16[2,768,256]{2,1,0:T(8,128)(2,1)S(1)} %copy-done.13), channel_id=1, source_target_pairs={{0,120},{8,16},{16,8},{24,32},{32,24},{40,48},{48,40},{56,64},{64,... | collective-permute-start | bytes 2359304 | tf_op jit(solution)/shard_map/ppermute | solution.py:41
  251.0 8.2 %collective-permute-start.26 = (bf16[2,2,12,768]{3,0,2,1:T(2,128)(2,1)S(1)}, bf16[2,2,12,768]{3,0,2,1:T(2,128)(2,1)S(1)}, u32[]{:S(2)}, u32[]{:S(2)}) collective-permute-start(bf16[2,2,12,768]{3,0,2,1:T(2,128)(2,1)S(1)} %fusion.5), channel_id=1, source_target_pairs={{0,3},{1,0},{2,1},{3,2},{4,7},{5,4},{6,5},{7,6},{8,11},{9,8},{10,9... | collective-permute-start | bytes 221192 | tf_op jit(solution)/shard_map/ppermute | solution.py:47
  (33 other events, 290.4 us)

commit v2 on v1

--- a/solution.py
+++ b/solution.py
@@ -16,10 +16,11 @@
 HEADS = 12
 FEATURES = HEADS * HEAD
 POOL = 3 * TILES
+HALF = FEATURES // 2
 SCALING = 1.0 / math.sqrt(HEAD)
 LOG2E = math.log2(math.e)
 GROUPS = (2, 4, 6)
-CALLS = ((0, 0, 2, 0), (1, 0, 4, 0), (2, 0, 4, 1), (2, 4, 2, 2))
+CALLS = ((0, 0, 2, 0), (1, 0, 4, 0), (2, 0, 6, 1))
 VMEM = 48 * 1024 * 1024
 F32 = jnp.float32
 BF16 = jnp.bfloat16
@@ -132,9 +133,8 @@
     accv[...] = jnp.zeros_like(accv)
     place = lax.broadcasted_iota(jnp.int32, (TILE, TILE), 0)
 
-    @pl.loop(0, TILES)
-    def _(tile):
-        rows = pl.ds(pl.multiple_of(tile * TILE, TILE), TILE)
+    for tile in range(TILES):
+        rows = slice(tile * TILE, (tile + 1) * TILE)
         q = q_ref[rows, :]
         g = g_ref[rows, :]
         codes = [codes_ref[tile, slot] for slot in range(SLOTS)]
@@ -183,20 +183,20 @@
             aliases[len(operands)] = index
             operands.append(array)
             in_specs.append(pl.BlockSpec(memory_space=pl.ANY))
-    whole = jax.ShapeDtypeStruct((ROWS, FEATURES), BF16)
+    at_half = pl.BlockSpec((ROWS, HEAD), lambda i: (0, first % 6 + i))
     macs = 6 * heads * TILES * TILE * SLOTS * TILE * HEAD
     return pl.pallas_call(
         attention_kernel,
         grid=(heads,),
         out_shape=[
-            whole,
-            whole,
+            jax.ShapeDtypeStruct((ROWS, FEATURES), BF16),
+            jax.ShapeDtypeStruct((ROWS, HALF), BF16),
             jax.ShapeDtypeStruct((2, ROWS, width), F32),
             jax.ShapeDtypeStruct((2, ROWS, width), BF16),
             jax.ShapeDtypeStruct((2, ROWS, width), BF16),
         ],
         in_specs=in_specs,
-        out_specs=[at_head, at_head, part, part, part],
+        out_specs=[at_head, at_half, part, part, part],
         scratch_shapes=[
             pltpu.VMEM((POOL, TILE, HEAD), BF16),
             pltpu.VMEM((POOL, TILE, HEAD), BF16),
@@ -246,40 +246,87 @@
     return lax.dynamic_index_in_dim(array, index, axis, keepdims=False)
 
 
-def weight_kernel(core_ref, rows_ref, att_ref, *refs):
-    for base, core in ((0, core_ref[0]), (2, 1 - core_ref[0])):
+def weight_kernel(core_ref, rows_ref, att_ref, keep_ref, send_ref):
+    for ref, core in ((keep_ref, core_ref[0]), (send_ref, 1 - core_ref[0])):
         rows = rows_ref[pl.ds(pl.multiple_of(core * 96, 96), 96), :]
-        for side in range(2):
-            cols = slice(side * 768, (side + 1) * 768)
-            ref = refs[base + side]
-            ref[0] = nn(rows, att_ref[:, cols]).astype(ref.dtype)
+        ref[0] = nn(rows, att_ref[...]).astype(ref.dtype)
 
 
 def weight_parts(core, rows_t, att):
-    block = pl.BlockSpec((1, 96, 768), lambda i: (i, 0, 0))
+    block = pl.BlockSpec((1, 96, HALF), lambda i: (i, 0, 0))
     return pl.pallas_call(
         weight_kernel,
         grid=(8,),
-        out_shape=[
-            jax.ShapeDtypeStruct((8, 96, 768), kind) for kind in (F32, F32, BF16, BF16)
-        ],
+        out_shape=[jax.ShapeDtypeStruct((8, 96, HALF), kind) for kind in (F32, BF16)],
         in_specs=[
             pl.BlockSpec(memory_space=pltpu.SMEM),
             pl.BlockSpec((192, ROWS), lambda i: (i, 0)),
-            pl.BlockSpec((ROWS, FEATURES), lambda i: (0, 0)),
+            pl.BlockSpec((ROWS, HALF), lambda i: (0, 0)),
         ],
-        out_specs=[block] * 4,
-        compiler_params=pltpu.CompilerParams(vmem_limit_bytes=VMEM),
-        cost_estimate=pl.CostEstimate(
-            flops=ROWS * FEATURES, bytes_accessed=1_000_000, transcendentals=0
+        out_specs=[block, block],
+        compiler_params=pltpu.CompilerParams(vmem_limit_bytes=VMEM),
+        cost_estimate=pl.CostEstimate(
+            flops=ROWS * HALF, bytes_accessed=500_000, transcendentals=0
         ),
         name="weight_parts",
     )(core, rows_t, att)
 
 
-def axis_sum(held, axis, index, shift):
-    got = [shift(picked(held, axis, (index + by) % 4).astype(BF16), by) for by in (1, 2, 3)]
-    return picked(held, axis, index) + sum(a.astype(F32) for a in got)
+def core_sum_kernel(z_ref, keep_ref, got_ref, *refs):
+    held = refs[4]
+    for high in range(2):
+        total = keep_ref[high] + got_ref[high].astype(F32)
+        for low in range(2):
+            for z in range(4):
+                row, place = low * 48 + z * 12, (high * 2 + low) * 12
+                by = lax.rem(z - z_ref[0] + 4, 4)
+                held[by, place : place + 12, :] = total[row : row + 12, :]
+    for by, ref in enumerate(refs[:4]):
+        ref[...] = held[by].astype(ref.dtype)
+
+
+def core_sum(z, keep, got):
+    block = pl.BlockSpec((2, 96, HALF), lambda i: (i, 0, 0))
+    return pl.pallas_call(
+        core_sum_kernel,
+        grid=(4,),
+        out_shape=[jax.ShapeDtypeStruct((192, HALF), kind) for kind in (F32, BF16, BF16, BF16)],
+        in_specs=[pl.BlockSpec(memory_space=pltpu.SMEM), block, block],
+        out_specs=[pl.BlockSpec((48, HALF), lambda i: (i, 0))] * 4,
+        scratch_shapes=[pltpu.VMEM((4, 48, HALF), F32)],
+        compiler_params=pltpu.CompilerParams(vmem_limit_bytes=VMEM),
+        cost_estimate=pl.CostEstimate(
+            flops=ROWS * HALF, bytes_accessed=500_000, transcendentals=0
+        ),
+        name="core_sum",
+    )(z, keep, got)
+
+
+def z_sum_kernel(y_ref, *refs):
+    outs, held = refs[8:12], refs[12]
+    for side in range(2):
+        own, got = refs[4 * side], refs[4 * side + 1 : 4 * side + 4]
+        cols = slice(side * HALF, (side + 1) * HALF)
+        held[:, cols] = own[...] + sum(ref[...].astype(F32) for ref in got)
+    for by, ref in enumerate(outs):
+        row = pl.multiple_of(lax.rem(y_ref[0] + by, 4) * 48, 48)
+        ref[...] = held[pl.ds(row, 48), :].astype(ref.dtype)
+
+
+def z_sum(y, sides):
+    whole = pl.BlockSpec(memory_space=pltpu.VMEM)
+    return pl.pallas_call(
+        z_sum_kernel,
+        out_shape=[jax.ShapeDtypeStruct((48, FEATURES), kind) for kind in (F32, BF16, BF16, BF16)],
+        in_specs=[pl.BlockSpec(memory_space=pltpu.SMEM)] + [whole] * 8,
+        out_specs=[whole] * 4,
+        scratch_shapes=[pltpu.VMEM((192, FEATURES), F32)],
+        compiler_params=pltpu.CompilerParams(vmem_limit_bytes=VMEM),
+        cost_estimate=pl.CostEstimate(
+            flops=ROWS * HALF, bytes_accessed=500_000, transcendentals=0
+        ),
+        name="z_sum",
+    )(y, *sides)
 
 
 def x_sum(held, tm, dp):
@@ -328,9 +375,9 @@
     leaving[2], arriving[0] = together((leaving[2], arriving[0]))
     arriving.append(outer_swap(leaving[2]))
     ki, vi = inner_swap(k), inner_swap(v)
-    ready, arriving[0] = together((tuple(mine), arriving[0]))
+    rows_t = together((rows_in, both))[0].T
+    ready, arriving[0], rows_t = together((tuple(mine), arriving[0], rows_t))
     theirs = [inner_swap(a) for a in ready]
-    rows_t = together(together((rows_in, both))[0].T)
     place = jnp.stack((z, core)).astype(jnp.int32)
     place, arriving[1] = together((place, arriving[1]))
     head_grad = project(place, rows_in, mine + theirs)
@@ -340,6 +387,9 @@
     inside, first, parts, firsts = 0, 0, [], []
     for group, skip, heads, which in CALLS:
         width = sum(call[2] for call in CALLS if call[3] == which) * HEAD
+        if first == 6:
+            att_a = held[1]
+            held = [held[0]] + [None] * 4
         held = attention(
             codes, lens, q, head_grad, k, v, ki, vi, arriving[group],
             first, skip, heads, inside, held, width,
@@ -347,33 +397,25 @@
         inside += heads
         first += heads
         if inside * HEAD == width:
-            parts.append((held[2], inner_swap(held[3]), outer_swap(held[4])))
+            parts.append([held[2], inner_swap(held[3]), outer_swap(held[4])])
             firsts.append(first - inside)
             held = list(held[:2]) + [None] * 3
             inside = 0
-    dq, att = held[:2]
-    keep_a, keep_b, send_a, send_b = weight_parts(place[1:], rows_t, att)
-    own, from_in, from_out = parts[0]
-    send_a, send_b, from_out = together((send_a, send_b, from_out))
-    parts[0] = (own, from_in, from_out)
-    y = tm // 4
-    late = (keep_b + inner_swap(send_b).astype(F32)).reshape(4, 2, 2, 4, 12, 768)
-    early = (keep_a + inner_swap(send_a).astype(F32)).reshape(4, 2, 96, 768)
-    early = axis_sum(early, 0, y, y_shift).reshape(2, 2, 4, 12, 768)
-    late = axis_sum(late, 3, z, z_shift)
-    own, from_in, from_out = parts[1]
-    early, late, from_out = together((early, late, from_out))
-    parts[1] = (own, from_in, from_out)
-    early = axis_sum(early, 2, z, z_shift)
-    late = axis_sum(late, 0, y, y_shift)
-    own, from_in, from_out = parts[2]
-    early, late, from_out = together((early, late, from_out))
-    parts[2] = (own, from_in, from_out)
-    weight_grad = x_sum(jnp.concatenate((early, late), axis=3), tm, dp)
-    grads = ()
-    for part, first in zip(parts, firsts):
-        grads = finish(*part, first, grads)
-    dk, dv = grads
+    dq, att_b = held[:2]
+    att_a, att_b = together((att_a, att_b))
+    keep_a, send_a = weight_parts(place[1:], rows_t, att_a)
+    sums_a = core_sum(place[:1], keep_a, inner_swap(send_a))
+    side_a = [sums_a[0]] + [z_shift(sums_a[by], by) for by in (1, 2, 3)]
+    keep_b, send_b = weight_parts(place[1:], rows_t, att_b)
+    send_b, parts[0][2] = together((send_b, parts[0][2]))
+    sums_b = core_sum(place[:1], keep_b, inner_swap(send_b))
+    side_b = [sums_b[0]] + [z_shift(sums_b[by], by) for by in (1, 2, 3)]
+    sums = z_sum((tm // 4).astype(jnp.int32)[None], side_a + side_b)
+    total = sums[0] + sum(y_shift(sums[by], by).astype(F32) for by in (1, 2, 3))
+    grads = finish(*parts[0], 0, ())
+    total, parts[1][2], *grads = together((total, parts[1][2], *grads))
+    weight_grad = x_sum(total.reshape(2, 2, 12, FEATURES), tm, dp)
+    dk, dv = finish(*parts[1], firsts[1], grads)
     return dq[None], dk[None], dv[None], weight_grad
 
 

time: 282 us -> 261 us (0.926); the launches traced: 277 us -> 260 us
  waiting for transfers between devices: 70.6 us -> 62.1 us
  other arithmetic: 10 us -> 4.23 us
  starting transfers between devices: 50.1 us -> 45.2 us
  Pallas kernels: 120 us -> 124 us
    ppermute x6 -> x3, waiting for transfers between devices: 14.6 us -> 0.45 us  [y_shift(): return lax.ppermute(a, 'tm', [(i, (i + 4 * by) % 16) for i in range(16)])]
    ppermute x9, waiting for transfers between devices: 35.8 us -> 44.8 us  [z_shift(): lax.ppermute(a, 'dp', [(i, i // 4 * 4 + (i + by) % 4) for i in range(8)])]
    ppermute x6 -> x5, starting transfers between devices: 23.2 us -> 15.7 us  [outer_swap(): lax.ppermute(a, 'tm', [(i, (i + 1) % 16 if i % 2 else (i - 1) % 16) for i...]
    add x5 -> x1, other arithmetic: 6.97 us -> 0.06 us  [shards(): sums[0] + sum((y_shift(sums[by], by).astype(F32) for by in (1, 2, 3)))]
    ppermute x9, starting transfers between devices: 15.1 us -> 19.8 us  [z_shift(): lax.ppermute(a, 'dp', [(i, i // 4 * 4 + (i + by) % 4) for i in range(8)])]
    pallas_call x1 -> x2, Pallas kernels: 10.8 us -> 14.4 us  [weight_parts(): pl.pallas_call(weight_kernel, grid=(8,), out_shape=[jax.ShapeDtypeStruct(...]
    another operation x6, local copies, waits for them, and re-layouts: 2.45 us -> 5.97 us  [outgoing(): return jnp.stack((k[:, cols], v[:, cols]))]
    unnamed x53 -> x47, local copies, waits for them, and re-layouts: 14.5 us -> 15.6 us
  transfers between devices with their start and end apart: 36 -> 31, of which waited for: 19 -> 13; matrix products, arithmetic and copies ran while one was open for 9% -> 6% of each run, Pallas kernels for 43% -> 48%
where the time goes in v2:
time: 261 us; the launch traced here: 260 us
  Pallas kernels  124 us (48%)
  waiting for transfers between devices  62.1 us (24%)
  starting transfers between devices  45.2 us (17%)
  local copies, waits for them, and re-layouts  23.3 us (9%)
  other arithmetic  4.23 us (2%)
    pallas_call x3, Pallas kernels, attention(): pl.pallas_call(attention_kernel, grid=(heads,), out_shape=[jax.ShapeDtype...  82.7 us
    ppermute x9, waiting for transfers between devices, z_shift(): lax.ppermute(a, 'dp', [(i, i // 4 * 4 + (i + by) % 4) for i in range(8)])  44.8 us
    ppermute x9, starting transfers between devices, z_shift(): lax.ppermute(a, 'dp', [(i, i // 4 * 4 + (i + by) % 4) for i in range(8)])  19.8 us
    ppermute x5, starting transfers between devices, outer_swap(): lax.ppermute(a, 'tm', [(i, (i + 1) % 16 if i % 2 else (i - 1) % 16) for i...  15.7 us
    unnamed x47, local copies, waits for them, and re-layouts  15.6 us
    pallas_call x2, Pallas kernels, weight_parts(): pl.pallas_call(weight_kernel, grid=(8,), out_shape=[jax.ShapeDtypeStruct(...  14.4 us
    pallas_call x2, Pallas kernels, finish(): pl.pallas_call(finish_kernel, grid=(width // step,), out_shape=[whole, wh...  10.7 us
    ppermute x5, waiting for transfers between devices, outer_swap(): lax.ppermute(a, 'tm', [(i, (i + 1) % 16 if i % 2 else (i - 1) % 16) for i...  10.4 us
  transfers between devices with their start and end apart: 31, of which 13 were waited for; matrix products, arithmetic and copies ran while one was open for 6% of the time, Pallas kernels for 48%

profile of v2, /device:TPU:0, one launch (start us, length us, event | category | flops | bytes accessed | tf_op | source)
XLA Modules:
  0.0 259.7 jit_solution(2730491596899355322)
XLA Ops:
  6.2 4.2 %collective-permute-done = bf16[96,1536]{1,0:T(8,128)(2,1)S(1)} collective-permute-done((bf16[96,1536]{1,0:T(8,128)(2,1)S(1)}, bf16[96,1536]{1,0:T(8,128)(2,1)S(1)}, u32[]{:S(2)}, u32[]{:S(2)}) %collective-permute-start) | collective-permute-done | bytes 294944 | tf_op jit(solution)/shard_map/ppermute | solution.py:52
  12.8 3.8 %collective-permute-start.5 = (bf16[2,768,256]{2,1,0:T(8,128)(2,1)S(1)}, bf16[2,768,256]{2,1,0:T(8,128)(2,1)S(1)}, u32[]{:S(2)}, u32[]{:S(2)}) collective-permute-start(bf16[2,768,256]{2,1,0:T(8,128)(2,1)S(1)} %pad_maximum_fusion.2), channel_id=1, source_target_pairs={{0,120},{8,16},{16,8},{24,32},{32,24},{40,48},{48,40},{56,64},{64,... | collective-permute-start | bytes 2359304 | tf_op jit(solution)/shard_map/ppermute | solution.py:42
  19.1 8.4 %collective-permute-done.1.refs_1_ = bf16[2,96,1536]{2,1,0:T(8,128)(2,1)} collective-permute-done((bf16[2,96,1536]{2,1,0:T(8,128)(2,1)S(1)}, bf16[2,96,1536]{2,1,0:T(8,128)(2,1)}, u32[]{:S(2)}, u32[]{:S(2)}) %collective-permute-start.1) | collective-permute-done | bytes 589856 | tf_op jit(solution)/shard_map/ppermute | solution.py:48
  27.5 3.4 %collective-permute-start.2 = (bf16[2,768,512]{2,1,0:T(8,128)(2,1)}, bf16[2,768,512]{2,1,0:T(8,128)(2,1)S(1)}, u32[]{:S(2)}, u32[]{:S(2)}) collective-permute-start(bf16[2,768,512]{2,1,0:T(8,128)(2,1)} %pad_maximum_fusion.1), channel_id=1, source_target_pairs={{0,120},{8,16},{16,8},{24,32},{32,24},{40,48},{48,40},{56,64},{64,... | collective-permute-start | bytes 4718600 | tf_op jit(solution)/shard_map/ppermute | solution.py:42
  32.2 3.7 %collective-permute-done.5.kvx = bf16[2,768,256]{2,1,0:T(8,128)(2,1)S(1)} collective-permute-done((bf16[2,768,256]{2,1,0:T(8,128)(2,1)S(1)}, bf16[2,768,256]{2,1,0:T(8,128)(2,1)S(1)}, u32[]{:S(2)}, u32[]{:S(2)}) %collective-permute-start.5) | collective-permute-done | bytes 786464 | tf_op jit(solution)/shard_map/ppermute | solution.py:42
  39.2 4.3 %copy.24 = bf16[1,768,1536]{1,2,0:T(8,128)(2,1)} copy(bf16[1,768,1536]{2,1,0:T(8,128)(2,1)} %param.11) | data formatting | bytes 4718592 | tf_op args[3]
  47.4 11.7 %collective-permute-done.4.refs_3_ = bf16[2,96,1536]{2,1,0:T(8,128)(2,1)} collective-permute-done((bf16[2,96,1536]{2,1,0:T(8,128)(2,1)S(1)}, bf16[2,96,1536]{2,1,0:T(8,128)(2,1)}, u32[]{:S(2)}, u32[]{:S(2)}) %collective-permute-start.4) | collective-permute-done | bytes 589856 | tf_op jit(solution)/shard_map/ppermute | solution.py:48
  63.0 6.6 %collective-permute-done.2.kvx = bf16[2,768,512]{2,1,0:T(8,128)(2,1)S(1)} collective-permute-done((bf16[2,768,512]{2,1,0:T(8,128)(2,1)}, bf16[2,768,512]{2,1,0:T(8,128)(2,1)S(1)}, u32[]{:S(2)}, u32[]{:S(2)}) %collective-permute-start.2) | collective-permute-done | bytes 1572896 | tf_op jit(solution)/shard_map/ppermute | solution.py:42
  70.0 3.1 %collective-permute-start.12 = (bf16[2,768,768]{2,1,0:T(8,128)(2,1)}, bf16[2,768,768]{2,1,0:T(8,128)(2,1)S(1)}, u32[]{:S(2)}, u32[]{:S(2)}) collective-permute-start(bf16[2,768,768]{2,1,0:T(8,128)(2,1)} %pad_maximum_fusion), channel_id=1, source_target_pairs={{0,120},{8,16},{16,8},{24,32},{32,24},{40,48},{48,40},{56,64},{64,... | collective-permute-start | bytes 7077896 | tf_op jit(solution)/shard_map/ppermute | solution.py:42
  74.2 10.0 %project.1.g_ref = bf16[768,1536]{1,0:T(8,128)(2,1)} custom-call(s32[2]{0:T(128)S(1)} %pad_add_fusion.1.place_ref, bf16[768,1536]{1,0:T(8,128)(2,1)} %bitcast.59, bf16[2,96,1536]{2,1,0:T(8,128)(2,1)S(1)} %pad_maximum_fusion.3.refs_0_, bf16[2,96,1536]{2,1,0:T(8,128)(2,1)} %collective-permute-done.1.refs_1_, ...), custom_call_target="tpu_custom_call" | custom-call | flops 1179648 | bytes 1000000 | tf_op jit(solution)/shard_map/project/pallas_call | solution.py:95
  84.3 15.0 %attention.3 = (bf16[768,1536]{1,0:T(8,128)(2,1)}, bf16[768,768]{1,0:T(8,128)(2,1)S(1)}, f32[2,768,768]{2,1,0:T(8,128)}, bf16[2,768,768]{2,1,0:T(8,128)(2,1)S(1)}, bf16[2,768,768]{2,1,0:T(8,128)(2,1)}) custom-call(s32[2,4]{1,0:T(2,128)S(1)} %get-tuple-element.126.codes_ref, s32[2,4]{1,0:T(2,128)S(1)} %select_reduce_fusion.lens_ref, ...), custom_call_target="tpu_custom_call" | custom-call | flops 28311552 | bytes 589824 | tf_op jit(solution)/shard_map/attention/pallas_call | solution.py:188
  99.2 27.7 %attention.4 = (bf16[768,1536]{1,0:T(8,128)(2,1)}, bf16[768,768]{1,0:T(8,128)(2,1)S(1)}, f32[2,768,768]{2,1,0:T(8,128)}, bf16[2,768,768]{2,1,0:T(8,128)(2,1)S(1)}, bf16[2,768,768]{2,1,0:T(8,128)(2,1)}) custom-call(s32[2,4]{1,0:T(2,128)S(1)} %get-tuple-element.126.codes_ref, ...), custom_call_target="tpu_custom_call", output_to_operand_aliasing={{0}: (9, {}), {1}: (10, {}), {2}: (11, {}), {3}: (12, {}), ... | custom-call | flops 56623104 | bytes 589824 | tf_op jit(solution)/shard_map/attention/pallas_call | solution.py:188
  126.9 2.5 collective-permute-start.18
  131.5 40.1 %attention.5 = (bf16[768,1536]{1,0:T(8,128)(2,1)}, bf16[768,768]{1,0:T(8,128)(2,1)S(1)}, f32[2,768,768]{2,1,0:T(8,128)}, bf16[2,768,768]{2,1,0:T(8,128)(2,1)}, bf16[2,768,768]{2,1,0:T(8,128)(2,1)}) custom-call(s32[2,4]{1,0:T(2,128)S(1)} %get-tuple-element.126.codes_ref, s32[2,4]{1,0:T(2,128)S(1)} %select_reduce_fusion.lens_ref, ...), custom_call_target="tpu_custom_call", output_to_operand_aliasing={{0}: (9, {})} | custom-call | flops 84934656 | bytes 589824 | tf_op jit(solution)/shard_map/attention/pallas_call | solution.py:188
  172.6 7.3 %weight_parts.2 = (f32[8,96,768]{2,1,0:T(8,128)S(1)}, bf16[8,96,768]{2,1,0:T(8,128)(2,1)S(1)}) custom-call(s32[1]{0:T(128)} %get-tuple-element.127.core_ref, bf16[1536,768]{1,0:T(8,128)(2,1)} %bitcast.56, bf16[768,768]{1,0:T(8,128)(2,1)S(1)} %get-tuple-element.88.att_ref), custom_call_target="tpu_custom_call" | custom-call | flops 589824 | bytes 500000 | tf_op jit(solution)/shard_map/weight_parts/pallas_call | solution.py:257
  180.5 7.2 %weight_parts.3 = (f32[8,96,768]{2,1,0:T(8,128)S(1)}, bf16[8,96,768]{2,1,0:T(8,128)(2,1)S(1)}) custom-call(s32[1]{0:T(128)} %get-tuple-element.127.core_ref, bf16[1536,768]{1,0:T(8,128)(2,1)} %bitcast.57, bf16[768,768]{1,0:T(8,128)(2,1)S(1)} %copy-done.5), custom_call_target="tpu_custom_call" | custom-call | flops 589824 | bytes 500000 | tf_op jit(solution)/shard_map/weight_parts/pallas_call | solution.py:257
  187.8 2.9 %collective-permute-start.26 = (bf16[2,768,768]{2,1,0:T(8,128)(2,1)}, bf16[2,768,768]{2,1,0:T(8,128)(2,1)}, u32[]{:S(2)}, u32[]{:S(2)}) collective-permute-start(bf16[2,768,768]{2,1,0:T(8,128)(2,1)} %get-tuple-element.108), channel_id=1, source_target_pairs={{0,120},{8,16},{16,8},{24,32},{32,24},{40,48},{48,40},{56,64},{64,... | collective-permute-start | bytes 7077896 | tf_op jit(solution)/shard_map/ppermute | solution.py:42
  198.3 4.3 %collective-permute-done.15.refs_1_ = bf16[192,768]{1,0:T(8,128)(2,1)S(1)} collective-permute-done((bf16[192,768]{1,0:T(8,128)(2,1)S(1)}, bf16[192,768]{1,0:T(8,128)(2,1)S(1)}, u32[]{:S(2)}, u32[]{:S(2)}) %collective-permute-start.15) | collective-permute-done | bytes 294944 | tf_op jit(solution)/shard_map/ppermute | solution.py:48
  204.3 5.4 %collective-permute-done.16.refs_2_ = bf16[192,768]{1,0:T(8,128)(2,1)S(1)} collective-permute-done((bf16[192,768]{1,0:T(8,128)(2,1)S(1)}, bf16[192,768]{1,0:T(8,128)(2,1)S(1)}, u32[]{:S(2)}, u32[]{:S(2)}) %collective-permute-start.16) | collective-permute-done | bytes 294944 | tf_op jit(solution)/shard_map/ppermute | solution.py:48
  212.1 8.3 %collective-permute-start.21 = (bf16[192,768]{1,0:T(8,128)(2,1)}, bf16[192,768]{1,0:T(8,128)(2,1)}, u32[]{:S(2)}, u32[]{:S(2)}) collective-permute-start(bf16[192,768]{1,0:T(8,128)(2,1)} %get-tuple-element.102), channel_id=1, source_target_pairs={{0,2},{1,3},{2,0},{3,1},{4,6},{5,7},{6,4},{7,5},{8,10},{9,11},{10,... | collective-permute-start | bytes 884744 | tf_op jit(solution)/shard_map/ppermute | solution.py:48
  220.4 5.5 %collective-permute-done.20.refs_5_ = bf16[192,768]{1,0:T(8,128)(2,1)S(1)} collective-permute-done((bf16[192,768]{1,0:T(8,128)(2,1)S(1)}, bf16[192,768]{1,0:T(8,128)(2,1)S(1)}, u32[]{:S(2)}, u32[]{:S(2)}) %collective-permute-start.20) | collective-permute-done | bytes 294944 | tf_op jit(solution)/shard_map/ppermute | solution.py:48
  226.7 7.0 %collective-permute-done.22.refs_7_ = bf16[192,768]{1,0:T(8,128)(2,1)} collective-permute-done((bf16[192,768]{1,0:T(8,128)(2,1)}, bf16[192,768]{1,0:T(8,128)(2,1)}, u32[]{:S(2)}, u32[]{:S(2)}) %collective-permute-start.22) | collective-permute-done | bytes 294944 | tf_op jit(solution)/shard_map/ppermute | solution.py:48
  243.5 5.1 %finish.2 = (bf16[768,1536]{1,0:T(8,128)(2,1)}, bf16[768,1536]{1,0:T(8,128)(2,1)}) custom-call(f32[2,768,768]{2,1,0:T(8,128)} %get-tuple-element.109.own_ref, bf16[2,768,768]{2,1,0:T(8,128)(2,1)} %collective-permute-done.27.in_ref, bf16[2,768,768]{2,1,0:T(8,128)(2,1)S(1)} %copy-done.1), custom_call_target="tpu_custom_call" | custom-call | flops 589824 | bytes 589824 | tf_op jit(solution)/shard_map/finish/pallas_call | solution.py:230
  253.4 5.6 %finish.3 = (bf16[768,1536]{1,0:T(8,128)(2,1)}, bf16[768,1536]{1,0:T(8,128)(2,1)}) custom-call(f32[2,768,768]{2,1,0:T(8,128)} %get-tuple-element.83.own_ref, bf16[2,768,768]{2,1,0:T(8,128)(2,1)} %collective-permute-done.13.in_ref, bf16[2,768,768]{2,1,0:T(8,128)(2,1)} %collective-permute-done.26.out_ref, ...), custom_call_target="tpu_custom_call", output_to_operand_aliasing={{0}: (3, {}), {1}: (4, {})} | custom-call | flops 589824 | bytes 589824 | tf_op jit(solution)/shard_map/finish/pallas_call | solution.py:230
  (117 shorter events, 55.6 us)
Async XLA Ops:
  3.4 80.9 %collective-permute-start.10 = (bf16[768,1536]{1,0:T(8,128)(2,1)}, bf16[768,1536]{1,0:T(8,128)(2,1)}, u32[]{:S(2)}, u32[]{:S(2)}) collective-permute-start(bf16[768,1536]{1,0:T(8,128)(2,1)} %bitcast.39), channel_id=1, source_target_pairs={{0,8},{8,0},{16,24},{24,16},{32,40},{40,32},{48,56},{56,48},{64,72... | collective-permute-start | bytes 7077896 | tf_op jit(solution)/shard_map/ppermute | solution.py:38
  3.4 80.9 %collective-permute-start.11 = (bf16[768,1536]{1,0:T(8,128)(2,1)}, bf16[768,1536]{1,0:T(8,128)(2,1)}, u32[]{:S(2)}, u32[]{:S(2)}) collective-permute-start(bf16[768,1536]{1,0:T(8,128)(2,1)} %bitcast.46), channel_id=1, source_target_pairs={{0,8},{8,0},{16,24},{24,16},{32,40},{40,32},{48,56},{56,48},{64,72... | collective-permute-start | bytes 7077896 | tf_op jit(solution)/shard_map/ppermute | solution.py:38
  10.5 16.9 %collective-permute-start.1 = (bf16[2,96,1536]{2,1,0:T(8,128)(2,1)S(1)}, bf16[2,96,1536]{2,1,0:T(8,128)(2,1)}, u32[]{:S(2)}, u32[]{:S(2)}) collective-permute-start(bf16[2,96,1536]{2,1,0:T(8,128)(2,1)S(1)} %pad_maximum_fusion.3.refs_0_), channel_id=1, source_target_pairs={{0,1},{1,2},{2,3},{3,0},{4,5},{5,6},{6,7},{7,4},{8,9},{9,10},{10,1... | collective-permute-start | bytes 1769480 | tf_op jit(solution)/shard_map/ppermute | solution.py:48
  12.8 23.1 %collective-permute-start.5 = (bf16[2,768,256]{2,1,0:T(8,128)(2,1)S(1)}, bf16[2,768,256]{2,1,0:T(8,128)(2,1)S(1)}, u32[]{:S(2)}, u32[]{:S(2)}) collective-permute-start(bf16[2,768,256]{2,1,0:T(8,128)(2,1)S(1)} %pad_maximum_fusion.2), channel_id=1, source_target_pairs={{0,120},{8,16},{16,8},{24,32},{32,24},{40,48},{48,40},{56,64},{64,... | collective-permute-start | bytes 2359304 | tf_op jit(solution)/shard_map/ppermute | solution.py:42
  27.5 42.1 %collective-permute-start.2 = (bf16[2,768,512]{2,1,0:T(8,128)(2,1)}, bf16[2,768,512]{2,1,0:T(8,128)(2,1)S(1)}, u32[]{:S(2)}, u32[]{:S(2)}) collective-permute-start(bf16[2,768,512]{2,1,0:T(8,128)(2,1)} %pad_maximum_fusion.1), channel_id=1, source_target_pairs={{0,120},{8,16},{16,8},{24,32},{32,24},{40,48},{48,40},{56,64},{64,... | collective-permute-start | bytes 4718600 | tf_op jit(solution)/shard_map/ppermute | solution.py:42
  30.9 16.6 %collective-permute-start.3 = (bf16[2,96,1536]{2,1,0:T(8,128)(2,1)S(1)}, bf16[2,96,1536]{2,1,0:T(8,128)(2,1)}, u32[]{:S(2)}, u32[]{:S(2)}) collective-permute-start(bf16[2,96,1536]{2,1,0:T(8,128)(2,1)S(1)} %pad_maximum_fusion.3.refs_0_), channel_id=1, source_target_pairs={{0,2},{1,3},{2,0},{3,1},{4,6},{5,7},{6,4},{7,5},{8,10},{9,11},{10,... | collective-permute-start | bytes 1769480 | tf_op jit(solution)/shard_map/ppermute | solution.py:48
  35.9 23.3 %collective-permute-start.4 = (bf16[2,96,1536]{2,1,0:T(8,128)(2,1)S(1)}, bf16[2,96,1536]{2,1,0:T(8,128)(2,1)}, u32[]{:S(2)}, u32[]{:S(2)}) collective-permute-start(bf16[2,96,1536]{2,1,0:T(8,128)(2,1)S(1)} %pad_maximum_fusion.3.refs_0_), channel_id=1, source_target_pairs={{0,3},{1,0},{2,1},{3,2},{4,7},{5,4},{6,5},{7,6},{8,11},{9,8},{10,9... | collective-permute-start | bytes 1769480 | tf_op jit(solution)/shard_map/ppermute | solution.py:48
  59.2 10.8 %collective-permute-start.7 = (bf16[2,96,1536]{2,1,0:T(8,128)(2,1)}, bf16[2,96,1536]{2,1,0:T(8,128)(2,1)}, u32[]{:S(2)}, u32[]{:S(2)}) collective-permute-start(bf16[2,96,1536]{2,1,0:T(8,128)(2,1)} %collective-permute-done.1.refs_1_), channel_id=1, source_target_pairs={{0,8},{8,0},{16,24},{24,16},{32,40},{40,32},{48,56},{56,48},{64,72... | collective-permute-start | bytes 1769480 | tf_op jit(solution)/shard_map/ppermute | solution.py:38
  62.8 10.3 %collective-permute-start.8 = (bf16[2,96,1536]{2,1,0:T(8,128)(2,1)}, bf16[2,96,1536]{2,1,0:T(8,128)(2,1)}, u32[]{:S(2)}, u32[]{:S(2)}) collective-permute-start(bf16[2,96,1536]{2,1,0:T(8,128)(2,1)} %collective-permute-done.3.refs_2_), channel_id=1, source_target_pairs={{0,8},{8,0},{16,24},{24,16},{32,40},{40,32},{48,56},{56,48},{64,72... | collective-permute-start | bytes 1769480 | tf_op jit(solution)/shard_map/ppermute | solution.py:38
  70.0 60.0 %collective-permute-start.12 = (bf16[2,768,768]{2,1,0:T(8,128)(2,1)}, bf16[2,768,768]{2,1,0:T(8,128)(2,1)S(1)}, u32[]{:S(2)}, u32[]{:S(2)}) collective-permute-start(bf16[2,768,768]{2,1,0:T(8,128)(2,1)} %pad_maximum_fusion), channel_id=1, source_target_pairs={{0,120},{8,16},{16,8},{24,32},{32,24},{40,48},{48,40},{56,64},{64,... | collective-permute-start | bytes 7077896 | tf_op jit(solution)/shard_map/ppermute | solution.py:42
  126.9 60.7 %collective-permute-start.18 = (bf16[2,768,768]{2,1,0:T(8,128)(2,1)}, bf16[2,768,768]{2,1,0:T(8,128)(2,1)S(1)}, u32[]{:S(2)}, u32[]{:S(2)}) collective-permute-start(bf16[2,768,768]{2,1,0:T(8,128)(2,1)} %get-tuple-element.98), channel_id=1, source_target_pairs={{0,120},{8,16},{16,8},{24,32},{32,24},{40,48},{48,40},{56,64},{64,... | collective-permute-start | bytes 7077896 | tf_op jit(solution)/shard_map/ppermute | solution.py:42
  129.5 110.6 %collective-permute-start.27 = (bf16[2,768,768]{2,1,0:T(8,128)(2,1)S(1)}, bf16[2,768,768]{2,1,0:T(8,128)(2,1)}, u32[]{:S(2)}, u32[]{:S(2)}) collective-permute-start(bf16[2,768,768]{2,1,0:T(8,128)(2,1)S(1)} %get-tuple-element.110), channel_id=1, source_target_pairs={{0,8},{8,0},{16,24},{24,16},{32,40},{40,32},{48,56},{56,48},{64,72... | collective-permute-start | bytes 7077896 | tf_op jit(solution)/shard_map/ppermute | solution.py:38
  179.9 10.8 %collective-permute-start.14 = (bf16[8,96,768]{2,1,0:T(8,128)(2,1)S(1)}, bf16[8,96,768]{2,1,0:T(8,128)(2,1)S(1)}, u32[]{:S(2)}, u32[]{:S(2)}) collective-permute-start(bf16[8,96,768]{2,1,0:T(8,128)(2,1)S(1)} %get-tuple-element.90), channel_id=1, source_target_pairs={{0,8},{8,0},{16,24},{24,16},{32,40},{40,32},{48,56},{56,48},{64,72... | collective-permute-start | bytes 3538952 | tf_op jit(solution)/shard_map/ppermute | solution.py:38
  187.8 61.3 %collective-permute-start.26 = (bf16[2,768,768]{2,1,0:T(8,128)(2,1)}, bf16[2,768,768]{2,1,0:T(8,128)(2,1)}, u32[]{:S(2)}, u32[]{:S(2)}) collective-permute-start(bf16[2,768,768]{2,1,0:T(8,128)(2,1)} %get-tuple-element.108), channel_id=1, source_target_pairs={{0,120},{8,16},{16,8},{24,32},{32,24},{40,48},{48,40},{56,64},{64,... | collective-permute-start | bytes 7077896 | tf_op jit(solution)/shard_map/ppermute | solution.py:42
  190.7 62.7 %collective-permute-start.13 = (bf16[2,768,768]{2,1,0:T(8,128)(2,1)}, bf16[2,768,768]{2,1,0:T(8,128)(2,1)}, u32[]{:S(2)}, u32[]{:S(2)}) collective-permute-start(bf16[2,768,768]{2,1,0:T(8,128)(2,1)} %get-tuple-element.84), channel_id=1, source_target_pairs={{0,8},{8,0},{16,24},{24,16},{32,40},{40,32},{48,56},{56,48},{64,72... | collective-permute-start | bytes 7077896 | tf_op jit(solution)/shard_map/ppermute | solution.py:38
  191.9 10.7 %collective-permute-start.15 = (bf16[192,768]{1,0:T(8,128)(2,1)S(1)}, bf16[192,768]{1,0:T(8,128)(2,1)S(1)}, u32[]{:S(2)}, u32[]{:S(2)}) collective-permute-start(bf16[192,768]{1,0:T(8,128)(2,1)S(1)} %get-tuple-element.92), channel_id=1, source_target_pairs={{0,1},{1,2},{2,3},{3,0},{4,5},{5,6},{6,7},{7,4},{8,9},{9,10},{10,1... | collective-permute-start | bytes 884744 | tf_op jit(solution)/shard_map/ppermute | solution.py:48
  193.9 15.8 %collective-permute-start.16 = (bf16[192,768]{1,0:T(8,128)(2,1)S(1)}, bf16[192,768]{1,0:T(8,128)(2,1)S(1)}, u32[]{:S(2)}, u32[]{:S(2)}) collective-permute-start(bf16[192,768]{1,0:T(8,128)(2,1)S(1)} %get-tuple-element.93), channel_id=1, source_target_pairs={{0,2},{1,3},{2,0},{3,1},{4,6},{5,7},{6,4},{7,5},{8,10},{9,11},{10,... | collective-permute-start | bytes 884744 | tf_op jit(solution)/shard_map/ppermute | solution.py:48
  209.7 16.3 %collective-permute-start.20 = (bf16[192,768]{1,0:T(8,128)(2,1)S(1)}, bf16[192,768]{1,0:T(8,128)(2,1)S(1)}, u32[]{:S(2)}, u32[]{:S(2)}) collective-permute-start(bf16[192,768]{1,0:T(8,128)(2,1)S(1)} %get-tuple-element.101), channel_id=1, source_target_pairs={{0,1},{1,2},{2,3},{3,0},{4,5},{5,6},{6,7},{7,4},{8,9},{9,10},{10,1... | collective-permute-start | bytes 884744 | tf_op jit(solution)/shard_map/ppermute | solution.py:48
  212.1 14.6 %collective-permute-start.21 = (bf16[192,768]{1,0:T(8,128)(2,1)}, bf16[192,768]{1,0:T(8,128)(2,1)}, u32[]{:S(2)}, u32[]{:S(2)}) collective-permute-start(bf16[192,768]{1,0:T(8,128)(2,1)} %get-tuple-element.102), channel_id=1, source_target_pairs={{0,2},{1,3},{2,0},{3,1},{4,6},{5,7},{6,4},{7,5},{8,10},{9,11},{10,... | collective-permute-start | bytes 884744 | tf_op jit(solution)/shard_map/ppermute | solution.py:48
  239.8 8.8 %collective-permute-start.25 = (bf16[48,1536]{1,0:T(8,128)(2,1)}, bf16[48,1536]{1,0:T(8,128)(2,1)S(1)}, u32[]{:S(2)}, u32[]{:S(2)}) collective-permute-start(bf16[48,1536]{1,0:T(8,128)(2,1)} %get-tuple-element.107), channel_id=1, source_target_pairs={{0,96},{8,104},{16,112},{24,120},{32,0},{40,8},{48,16},{56,24},{64... | collective-permute-start | bytes 442376 | tf_op jit(solution)/shard_map/ppermute | solution.py:56
  239.8 8.8 %collective-permute-start.24 = (bf16[48,1536]{1,0:T(8,128)(2,1)}, bf16[48,1536]{1,0:T(8,128)(2,1)S(1)}, u32[]{:S(2)}, u32[]{:S(2)}) collective-permute-start(bf16[48,1536]{1,0:T(8,128)(2,1)} %get-tuple-element.106), channel_id=1, source_target_pairs={{0,64},{8,72},{16,80},{24,88},{32,96},{40,104},{48,112},{56,120},{... | collective-permute-start | bytes 442376 | tf_op jit(solution)/shard_map/ppermute | solution.py:56
  240.0 9.0 %collective-permute-start.23 = (bf16[48,1536]{1,0:T(8,128)(2,1)}, bf16[48,1536]{1,0:T(8,128)(2,1)S(1)}, u32[]{:S(2)}, u32[]{:S(2)}) collective-permute-start(bf16[48,1536]{1,0:T(8,128)(2,1)} %get-tuple-element.105), channel_id=1, source_target_pairs={{0,32},{8,40},{16,48},{24,56},{32,64},{40,72},{48,80},{56,88},{64,... | collective-permute-start | bytes 442376 | tf_op jit(solution)/shard_map/ppermute | solution.py:56
  249.2 9.8 %collective-permute-start.30 = (bf16[12,1536]{1,0:T(8,128)(2,1)S(1)}, bf16[12,1536]{1,0:T(8,128)(2,1)S(1)}, u32[]{:S(2)}, u32[]{:S(2)}) collective-permute-start(bf16[12,1536]{1,0:T(8,128)(2,1)S(1)} %get-tuple-element.123), channel_id=1, source_target_pairs={{0,20},{1,21},{2,22},{3,23},{4,16},{5,17},{6,18},{7,19},{8,28},{9,... | collective-permute-start | bytes 110600 | tf_op jit(solution)/shard_map/ppermute | solution.py:66
  250.1 8.9 %collective-permute-start.29 = (bf16[12,1536]{1,0:T(8,128)(2,1)S(1)}, bf16[12,1536]{1,0:T(8,128)(2,1)S(1)}, u32[]{:S(2)}, u32[]{:S(2)}) collective-permute-start(bf16[12,1536]{1,0:T(8,128)(2,1)S(1)} %get-tuple-element.124), channel_id=1, source_target_pairs={{0,16},{1,17},{2,18},{3,19},{4,20},{5,21},{6,22},{7,23},{8,24},{9,... | collective-permute-start | bytes 110600 | tf_op jit(solution)/shard_map/ppermute | solution.py:66
  (30 other events, 216.2 us)

commit v3 on v2

--- a/solution.py
+++ b/solution.py
@@ -150,17 +150,20 @@
         inverse = 1.0 / total
         probs = [e * inverse for e in powers]
         weights = [p.astype(BF16) for p in probs]
-        att = sum(nn(vt[codes[slot]], weights[slot]) for slot in range(SLOTS)).astype(BF16)
+        every = jnp.concatenate(weights, axis=0)
+        att = nn(jnp.concatenate([vt[code] for code in codes], axis=1), every).astype(BF16)
         att_ref[rows, :] = att.T
         rowdot = jnp.sum(g.T.astype(F32) * att.astype(F32), axis=0, keepdims=True)
-        dq = jnp.zeros((HEAD, TILE), F32)
+        dscores = []
         for slot in range(SLOTS):
             code = codes[slot]
             prob_grad = nt(vp[code], g)
             dscore = (probs[slot] * (prob_grad - rowdot)).astype(BF16)
-            dq += nn(kt[code], dscore)
+            dscores.append(dscore)
             acck[code] += nn(dscore, q)
             accv[code] += nn(weights[slot], g)
+        every = jnp.concatenate(dscores, axis=0)
+        dq = nn(jnp.concatenate([kt[code] for code in codes], axis=1), every)
         dq_ref[rows, :] = (dq * SCALING).astype(BF16).T
 
     for tile in range(TILES):
@@ -246,24 +249,28 @@
     return lax.dynamic_index_in_dim(array, index, axis, keepdims=False)
 
 
-def weight_kernel(core_ref, rows_ref, att_ref, keep_ref, send_ref):
+def weight_kernel(core_ref, rows_ref, att_ref, keep_ref, send_ref, held):
+    for part in range(4):
+        rows = slice(part * 384, (part + 1) * 384)
+        held[2 * part : 2 * part + 2] = nn(rows_ref[rows, :], att_ref[...]).reshape(2, 192, 256)
     for ref, core in ((keep_ref, core_ref[0]), (send_ref, 1 - core_ref[0])):
-        rows = rows_ref[pl.ds(pl.multiple_of(core * 96, 96), 96), :]
-        ref[0] = nn(rows, att_ref[...]).astype(ref.dtype)
+        rows = pl.ds(pl.multiple_of(core * 96, 96), 96)
+        ref[...] = held[:, rows, :].astype(ref.dtype)
 
 
 def weight_parts(core, rows_t, att):
-    block = pl.BlockSpec((1, 96, HALF), lambda i: (i, 0, 0))
+    block = pl.BlockSpec((8, 96, 256), lambda i: (0, 0, i))
     return pl.pallas_call(
         weight_kernel,
-        grid=(8,),
+        grid=(HALF // 256,),
         out_shape=[jax.ShapeDtypeStruct((8, 96, HALF), kind) for kind in (F32, BF16)],
         in_specs=[
             pl.BlockSpec(memory_space=pltpu.SMEM),
-            pl.BlockSpec((192, ROWS), lambda i: (i, 0)),
-            pl.BlockSpec((ROWS, HALF), lambda i: (0, 0)),
+            pl.BlockSpec((FEATURES, ROWS), lambda i: (0, 0)),
+            pl.BlockSpec((ROWS, 256), lambda i: (0, i)),
         ],
         out_specs=[block, block],
+        scratch_shapes=[pltpu.VMEM((8, 192, 256), F32)],
         compiler_params=pltpu.CompilerParams(vmem_limit_bytes=VMEM),
         cost_estimate=pl.CostEstimate(
             flops=ROWS * HALF, bytes_accessed=500_000, transcendentals=0
@@ -410,10 +417,11 @@
     send_b, parts[0][2] = together((send_b, parts[0][2]))
     sums_b = core_sum(place[:1], keep_b, inner_swap(send_b))
     side_b = [sums_b[0]] + [z_shift(sums_b[by], by) for by in (1, 2, 3)]
+    grads = finish(*parts[0], 0, ())
+    side_a[0], *grads = together((side_a[0], *grads))
     sums = z_sum((tm // 4).astype(jnp.int32)[None], side_a + side_b)
     total = sums[0] + sum(y_shift(sums[by], by).astype(F32) for by in (1, 2, 3))
-    grads = finish(*parts[0], 0, ())
-    total, parts[1][2], *grads = together((total, parts[1][2], *grads))
+    total, parts[1][2] = together((total, parts[1][2]))
     weight_grad = x_sum(total.reshape(2, 2, 12, FEATURES), tm, dp)
     dk, dv = finish(*parts[1], firsts[1], grads)
     return dq[None], dk[None], dv[None], weight_grad

time: 261 us -> 249 us (0.954)
  Pallas kernels: 124 us -> 113 us
  starting transfers between devices: 45.2 us -> 41.2 us
    ppermute x9, waiting for transfers between devices: 44.8 us -> 29.1 us  [z_shift(): lax.ppermute(a, 'dp', [(i, i // 4 * 4 + (i + by) % 4) for i in range(8)])]
    ppermute x3, waiting for transfers between devices: 0.45 us -> 14.4 us  [y_shift(): return lax.ppermute(a, 'tm', [(i, (i + 4 * by) % 16) for i in range(16)])]
    pallas_call x3, Pallas kernels: 82.7 us -> 76.6 us  [attention(): pl.pallas_call(attention_kernel, grid=(heads,), out_shape=[jax.ShapeDtype...]
    pallas_call x2, Pallas kernels: 14.4 us -> 10.7 us  [weight_parts(): pl.pallas_call(weight_kernel, grid=(HALF // 256,), out_shape=[jax.ShapeDt...]
    unnamed x47 -> x45, local copies, waits for them, and re-layouts: 15.6 us -> 16.9 us
  transfers between devices with their start and end apart: 31 -> 31, of which waited for: 13 -> 16; matrix products, arithmetic and copies ran while one was open for 6% -> 6% of each run, Pallas kernels for 48% -> 46%
where the time goes in v3:
time: 249 us; the launch traced here: 248 us
  Pallas kernels  113 us (45%)
  waiting for transfers between devices  62.7 us (25%)
  starting transfers between devices  41.2 us (17%)
  local copies, waits for them, and re-layouts  24.5 us (10%)
  other arithmetic  5.19 us (2%)
    pallas_call x3, Pallas kernels, attention(): pl.pallas_call(attention_kernel, grid=(heads,), out_shape=[jax.ShapeDtype...  76.6 us
    ppermute x9, waiting for transfers between devices, z_shift(): lax.ppermute(a, 'dp', [(i, i // 4 * 4 + (i + by) % 4) for i in range(8)])  29.1 us
    ppermute x9, starting transfers between devices, z_shift(): lax.ppermute(a, 'dp', [(i, i // 4 * 4 + (i + by) % 4) for i in range(8)])  17.7 us
    unnamed x45, local copies, waits for them, and re-layouts  16.9 us
    ppermute x3, waiting for transfers between devices, y_shift(): return lax.ppermute(a, 'tm', [(i, (i + 4 * by) % 16) for i in range(16)])  14.4 us
    ppermute x5, starting transfers between devices, outer_swap(): lax.ppermute(a, 'tm', [(i, (i + 1) % 16 if i % 2 else (i - 1) % 16) for i...  14.3 us
    ppermute x5, waiting for transfers between devices, outer_swap(): lax.ppermute(a, 'tm', [(i, (i + 1) % 16 if i % 2 else (i - 1) % 16) for i...  12.6 us
    pallas_call x2, Pallas kernels, weight_parts(): pl.pallas_call(weight_kernel, grid=(HALF // 256,), out_shape=[jax.ShapeDt...  10.7 us
  transfers between devices with their start and end apart: 31, of which 16 were waited for; matrix products, arithmetic and copies ran while one was open for 6% of the time, Pallas kernels for 46%

profile of v3, /device:TPU:0, one launch (start us, length us, event | category | flops | bytes accessed | tf_op | source)
XLA Modules:
  0.0 247.9 jit_solution(4914279365737842295)
XLA Ops:
  6.2 4.2 %collective-permute-done = bf16[96,1536]{1,0:T(8,128)(2,1)S(1)} collective-permute-done((bf16[96,1536]{1,0:T(8,128)(2,1)S(1)}, bf16[96,1536]{1,0:T(8,128)(2,1)S(1)}, u32[]{:S(2)}, u32[]{:S(2)}) %collective-permute-start) | collective-permute-done | bytes 294944 | tf_op jit(solution)/shard_map/ppermute | solution.py:52
  12.8 3.8 %collective-permute-start.5 = (bf16[2,768,256]{2,1,0:T(8,128)(2,1)S(1)}, bf16[2,768,256]{2,1,0:T(8,128)(2,1)S(1)}, u32[]{:S(2)}, u32[]{:S(2)}) collective-permute-start(bf16[2,768,256]{2,1,0:T(8,128)(2,1)S(1)} %pad_maximum_fusion.2), channel_id=1, source_target_pairs={{0,120},{8,16},{16,8},{24,32},{32,24},{40,48},{48,40},{56,64},{64,... | collective-permute-start | bytes 2359304 | tf_op jit(solution)/shard_map/ppermute | solution.py:42
  19.1 8.3 %collective-permute-done.1.refs_1_ = bf16[2,96,1536]{2,1,0:T(8,128)(2,1)S(1)} collective-permute-done((bf16[2,96,1536]{2,1,0:T(8,128)(2,1)S(1)}, bf16[2,96,1536]{2,1,0:T(8,128)(2,1)S(1)}, u32[]{:S(2)}, u32[]{:S(2)}) %collective-permute-start.1) | collective-permute-done | bytes 589856 | tf_op jit(solution)/shard_map/ppermute | solution.py:48
  27.4 3.4 %collective-permute-start.2 = (bf16[2,768,512]{2,1,0:T(8,128)(2,1)}, bf16[2,768,512]{2,1,0:T(8,128)(2,1)S(1)}, u32[]{:S(2)}, u32[]{:S(2)}) collective-permute-start(bf16[2,768,512]{2,1,0:T(8,128)(2,1)} %pad_maximum_fusion.1), channel_id=1, source_target_pairs={{0,120},{8,16},{16,8},{24,32},{32,24},{40,48},{48,40},{56,64},{64,... | collective-permute-start | bytes 4718600 | tf_op jit(solution)/shard_map/ppermute | solution.py:42
  32.1 3.8 %collective-permute-done.5.kvx = bf16[2,768,256]{2,1,0:T(8,128)(2,1)S(1)} collective-permute-done((bf16[2,768,256]{2,1,0:T(8,128)(2,1)S(1)}, bf16[2,768,256]{2,1,0:T(8,128)(2,1)S(1)}, u32[]{:S(2)}, u32[]{:S(2)}) %collective-permute-start.5) | collective-permute-done | bytes 786464 | tf_op jit(solution)/shard_map/ppermute | solution.py:42
  39.2 4.3 %copy.24 = bf16[1,768,1536]{1,2,0:T(8,128)(2,1)} copy(bf16[1,768,1536]{2,1,0:T(8,128)(2,1)} %param.11) | data formatting | bytes 4718592 | tf_op args[3]
  47.3 11.8 %collective-permute-done.4.refs_3_ = bf16[2,96,1536]{2,1,0:T(8,128)(2,1)} collective-permute-done((bf16[2,96,1536]{2,1,0:T(8,128)(2,1)S(1)}, bf16[2,96,1536]{2,1,0:T(8,128)(2,1)}, u32[]{:S(2)}, u32[]{:S(2)}) %collective-permute-start.4) | collective-permute-done | bytes 589856 | tf_op jit(solution)/shard_map/ppermute | solution.py:48
  62.9 6.8 %collective-permute-done.2.kvx = bf16[2,768,512]{2,1,0:T(8,128)(2,1)S(1)} collective-permute-done((bf16[2,768,512]{2,1,0:T(8,128)(2,1)}, bf16[2,768,512]{2,1,0:T(8,128)(2,1)S(1)}, u32[]{:S(2)}, u32[]{:S(2)}) %collective-permute-start.2) | collective-permute-done | bytes 1572896 | tf_op jit(solution)/shard_map/ppermute | solution.py:42
  70.0 2.9 %collective-permute-start.12 = (bf16[2,768,768]{2,1,0:T(8,128)(2,1)}, bf16[2,768,768]{2,1,0:T(8,128)(2,1)S(1)}, u32[]{:S(2)}, u32[]{:S(2)}) collective-permute-start(bf16[2,768,768]{2,1,0:T(8,128)(2,1)} %pad_maximum_fusion), channel_id=1, source_target_pairs={{0,120},{8,16},{16,8},{24,32},{32,24},{40,48},{48,40},{56,64},{64,... | collective-permute-start | bytes 7077896 | tf_op jit(solution)/shard_map/ppermute | solution.py:42
  74.0 10.0 %project.1.g_ref = bf16[768,1536]{1,0:T(8,128)(2,1)} custom-call(s32[2]{0:T(128)S(1)} %pad_add_fusion.1.place_ref, bf16[768,1536]{1,0:T(8,128)(2,1)} %bitcast.59, bf16[2,96,1536]{2,1,0:T(8,128)(2,1)S(1)} %pad_maximum_fusion.3.refs_0_, bf16[2,96,1536]{2,1,0:T(8,128)(2,1)S(1)} %collective-permute-done.1.refs_1_, ...), custom_call_target="tpu_custom_call" | custom-call | flops 1179648 | bytes 1000000 | tf_op jit(solution)/shard_map/project/pallas_call | solution.py:95
  84.0 13.9 %attention.3 = (bf16[768,1536]{1,0:T(8,128)(2,1)}, bf16[768,768]{1,0:T(8,128)(2,1)S(1)}, f32[2,768,768]{2,1,0:T(8,128)}, bf16[2,768,768]{2,1,0:T(8,128)(2,1)S(1)}, bf16[2,768,768]{2,1,0:T(8,128)(2,1)}) custom-call(s32[2,4]{1,0:T(2,128)S(1)} %get-tuple-element.128.codes_ref, s32[2,4]{1,0:T(2,128)S(1)} %select_reduce_fusion.lens_ref, ...), custom_call_target="tpu_custom_call" | custom-call | flops 28311552 | bytes 589824 | tf_op jit(solution)/shard_map/attention/pallas_call | solution.py:191
  97.9 25.6 %attention.4 = (bf16[768,1536]{1,0:T(8,128)(2,1)}, bf16[768,768]{1,0:T(8,128)(2,1)S(1)}, f32[2,768,768]{2,1,0:T(8,128)}, bf16[2,768,768]{2,1,0:T(8,128)(2,1)S(1)}, bf16[2,768,768]{2,1,0:T(8,128)(2,1)}) custom-call(s32[2,4]{1,0:T(2,128)S(1)} %get-tuple-element.128.codes_ref, ...), custom_call_target="tpu_custom_call", output_to_operand_aliasing={{0}: (9, {}), {1}: (10, {}), {2}: (11, {}), {3}: (12, {}), ... | custom-call | flops 56623104 | bytes 589824 | tf_op jit(solution)/shard_map/attention/pallas_call | solution.py:191
  128.4 37.1 %attention.5 = (bf16[768,1536]{1,0:T(8,128)(2,1)}, bf16[768,768]{1,0:T(8,128)(2,1)S(1)}, f32[2,768,768]{2,1,0:T(8,128)}, bf16[2,768,768]{2,1,0:T(8,128)(2,1)S(1)}, bf16[2,768,768]{2,1,0:T(8,128)(2,1)S(1)}) custom-call(s32[2,4]{1,0:T(2,128)S(1)} %get-tuple-element.128.codes_ref, ...), custom_call_target="tpu_custom_call", output_to_operand_aliasing={{0}: (9, {})} | custom-call | flops 84934656 | bytes 589824 | tf_op jit(solution)/shard_map/attention/pallas_call | solution.py:191
  166.8 5.4 %weight_parts.2 = (f32[8,96,768]{2,1,0:T(8,128)S(1)}, bf16[8,96,768]{2,1,0:T(8,128)(2,1)S(1)}) custom-call(s32[1]{0:T(128)} %get-tuple-element.129.core_ref, bf16[1536,768]{1,0:T(8,128)(2,1)} %bitcast.56, bf16[768,768]{1,0:T(8,128)(2,1)S(1)} %get-tuple-element.89.att_ref), custom_call_target="tpu_custom_call" | custom-call | flops 589824 | bytes 500000 | tf_op jit(solution)/shard_map/weight_parts/pallas_call | solution.py:263
  172.4 5.3 %weight_parts.3 = (f32[8,96,768]{2,1,0:T(8,128)S(1)}, bf16[8,96,768]{2,1,0:T(8,128)(2,1)S(1)}) custom-call(s32[1]{0:T(128)} %get-tuple-element.129.core_ref, bf16[1536,768]{1,0:T(8,128)(2,1)} %bitcast.57, bf16[768,768]{1,0:T(8,128)(2,1)S(1)} %get-tuple-element.95.att_ref), custom_call_target="tpu_custom_call" | custom-call | flops 589824 | bytes 500000 | tf_op jit(solution)/shard_map/weight_parts/pallas_call | solution.py:263
  189.1 2.5 %collective-permute-start.19 = (bf16[192,768]{1,0:T(8,128)(2,1)S(1)}, bf16[192,768]{1,0:T(8,128)(2,1)S(1)}, u32[]{:S(2)}, u32[]{:S(2)}) collective-permute-start(bf16[192,768]{1,0:T(8,128)(2,1)S(1)} %get-tuple-element.104), channel_id=1, source_target_pairs={{0,3},{1,0},{2,1},{3,2},{4,7},{5,4},{6,5},{7,6},{8,11},{9,8},{10,9... | collective-permute-start | bytes 884744 | tf_op jit(solution)/shard_map/ppermute | solution.py:48
  197.9 5.4 %collective-permute-done.18.refs_2_ = bf16[192,768]{1,0:T(8,128)(2,1)S(1)} collective-permute-done((bf16[192,768]{1,0:T(8,128)(2,1)S(1)}, bf16[192,768]{1,0:T(8,128)(2,1)S(1)}, u32[]{:S(2)}, u32[]{:S(2)}) %collective-permute-start.18) | collective-permute-done | bytes 294944 | tf_op jit(solution)/shard_map/ppermute | solution.py:48
  206.7 2.6 %collective-permute-start.23 = (bf16[192,768]{1,0:T(8,128)(2,1)}, bf16[192,768]{1,0:T(8,128)(2,1)}, u32[]{:S(2)}, u32[]{:S(2)}) collective-permute-start(bf16[192,768]{1,0:T(8,128)(2,1)} %get-tuple-element.110), channel_id=1, source_target_pairs={{0,3},{1,0},{2,1},{3,2},{4,7},{5,4},{6,5},{7,6},{8,11},{9,8},{10,9... | collective-permute-start | bytes 884744 | tf_op jit(solution)/shard_map/ppermute | solution.py:48
  211.0 5.1 %finish.2 = (bf16[768,1536]{1,0:T(8,128)(2,1)}, bf16[768,1536]{1,0:T(8,128)(2,1)}) custom-call(f32[2,768,768]{2,1,0:T(8,128)} %get-tuple-element.93.own_ref, bf16[2,768,768]{2,1,0:T(8,128)(2,1)} %collective-permute-done.15.in_ref, bf16[2,768,768]{2,1,0:T(8,128)(2,1)S(1)} %copy-done.3), custom_call_target="tpu_custom_call" | custom-call | flops 589824 | bytes 589824 | tf_op jit(solution)/shard_map/finish/pallas_call | solution.py:233
  222.4 3.3 %collective-permute-done.26 = bf16[48,1536]{1,0:T(8,128)(2,1)S(1)} collective-permute-done((bf16[48,1536]{1,0:T(8,128)(2,1)}, bf16[48,1536]{1,0:T(8,128)(2,1)S(1)}, u32[]{:S(2)}, u32[]{:S(2)}) %collective-permute-start.26) | collective-permute-done | bytes 147488 | tf_op jit(solution)/shard_map/ppermute | solution.py:56
  225.8 6.4 %collective-permute-done.25 = bf16[48,1536]{1,0:T(8,128)(2,1)S(1)} collective-permute-done((bf16[48,1536]{1,0:T(8,128)(2,1)}, bf16[48,1536]{1,0:T(8,128)(2,1)S(1)}, u32[]{:S(2)}, u32[]{:S(2)}) %collective-permute-start.25) | collective-permute-done | bytes 147488 | tf_op jit(solution)/shard_map/ppermute | solution.py:56
  232.1 4.7 %collective-permute-done.24 = bf16[48,1536]{1,0:T(8,128)(2,1)S(1)} collective-permute-done((bf16[48,1536]{1,0:T(8,128)(2,1)}, bf16[48,1536]{1,0:T(8,128)(2,1)S(1)}, u32[]{:S(2)}, u32[]{:S(2)}) %collective-permute-start.24) | collective-permute-done | bytes 147488 | tf_op jit(solution)/shard_map/ppermute | solution.py:56
  238.1 3.0 %collective-permute-start.29 = (bf16[12,1536]{1,0:T(8,128)(2,1)S(1)}, bf16[12,1536]{1,0:T(8,128)(2,1)S(1)}, u32[]{:S(2)}, u32[]{:S(2)}) collective-permute-start(bf16[12,1536]{1,0:T(8,128)(2,1)S(1)} %get-tuple-element.126), channel_id=1, source_target_pairs={{0,16},{1,17},{2,18},{3,19},{4,20},{5,21},{6,22},{7,23},{8,24},{9,... | collective-permute-start | bytes 110600 | tf_op jit(solution)/shard_map/ppermute | solution.py:66
  242.2 5.1 %finish.3 = (bf16[768,1536]{1,0:T(8,128)(2,1)}, bf16[768,1536]{1,0:T(8,128)(2,1)}) custom-call(f32[2,768,768]{2,1,0:T(8,128)} %get-tuple-element.84.own_ref, bf16[2,768,768]{2,1,0:T(8,128)(2,1)} %collective-permute-done.13.in_ref, bf16[2,768,768]{2,1,0:T(8,128)(2,1)S(1)} %collective-permute-done.27.out_ref, ...), custom_call_target="tpu_custom_call", output_to_operand_aliasing={{0}: (3, {}), {1}: (4, {})} | custom-call | flops 589824 | bytes 589824 | tf_op jit(solution)/shard_map/finish/pallas_call | solution.py:233
  (115 shorter events, 62.4 us)
Async XLA Ops:
  3.4 80.6 %collective-permute-start.10 = (bf16[768,1536]{1,0:T(8,128)(2,1)}, bf16[768,1536]{1,0:T(8,128)(2,1)}, u32[]{:S(2)}, u32[]{:S(2)}) collective-permute-start(bf16[768,1536]{1,0:T(8,128)(2,1)} %bitcast.39), channel_id=1, source_target_pairs={{0,8},{8,0},{16,24},{24,16},{32,40},{40,32},{48,56},{56,48},{64,72... | collective-permute-start | bytes 7077896 | tf_op jit(solution)/shard_map/ppermute | solution.py:38
  3.4 80.6 %collective-permute-start.11 = (bf16[768,1536]{1,0:T(8,128)(2,1)}, bf16[768,1536]{1,0:T(8,128)(2,1)}, u32[]{:S(2)}, u32[]{:S(2)}) collective-permute-start(bf16[768,1536]{1,0:T(8,128)(2,1)} %bitcast.46), channel_id=1, source_target_pairs={{0,8},{8,0},{16,24},{24,16},{32,40},{40,32},{48,56},{56,48},{64,72... | collective-permute-start | bytes 7077896 | tf_op jit(solution)/shard_map/ppermute | solution.py:38
  10.5 16.8 %collective-permute-start.1 = (bf16[2,96,1536]{2,1,0:T(8,128)(2,1)S(1)}, bf16[2,96,1536]{2,1,0:T(8,128)(2,1)S(1)}, u32[]{:S(2)}, u32[]{:S(2)}) collective-permute-start(bf16[2,96,1536]{2,1,0:T(8,128)(2,1)S(1)} %pad_maximum_fusion.3.refs_0_), channel_id=1, source_target_pairs={{0,1},{1,2},{2,3},{3,0},{4,5},{5,6},{6,7},{7,4},{8,9},{9,10},{10,1... | collective-permute-start | bytes 1769480 | tf_op jit(solution)/shard_map/ppermute | solution.py:48
  12.8 23.1 %collective-permute-start.5 = (bf16[2,768,256]{2,1,0:T(8,128)(2,1)S(1)}, bf16[2,768,256]{2,1,0:T(8,128)(2,1)S(1)}, u32[]{:S(2)}, u32[]{:S(2)}) collective-permute-start(bf16[2,768,256]{2,1,0:T(8,128)(2,1)S(1)} %pad_maximum_fusion.2), channel_id=1, source_target_pairs={{0,120},{8,16},{16,8},{24,32},{32,24},{40,48},{48,40},{56,64},{64,... | collective-permute-start | bytes 2359304 | tf_op jit(solution)/shard_map/ppermute | solution.py:42
  27.4 42.3 %collective-permute-start.2 = (bf16[2,768,512]{2,1,0:T(8,128)(2,1)}, bf16[2,768,512]{2,1,0:T(8,128)(2,1)S(1)}, u32[]{:S(2)}, u32[]{:S(2)}) collective-permute-start(bf16[2,768,512]{2,1,0:T(8,128)(2,1)} %pad_maximum_fusion.1), channel_id=1, source_target_pairs={{0,120},{8,16},{16,8},{24,32},{32,24},{40,48},{48,40},{56,64},{64,... | collective-permute-start | bytes 4718600 | tf_op jit(solution)/shard_map/ppermute | solution.py:42
  30.8 16.6 %collective-permute-start.3 = (bf16[2,96,1536]{2,1,0:T(8,128)(2,1)S(1)}, bf16[2,96,1536]{2,1,0:T(8,128)(2,1)}, u32[]{:S(2)}, u32[]{:S(2)}) collective-permute-start(bf16[2,96,1536]{2,1,0:T(8,128)(2,1)S(1)} %pad_maximum_fusion.3.refs_0_), channel_id=1, source_target_pairs={{0,2},{1,3},{2,0},{3,1},{4,6},{5,7},{6,4},{7,5},{8,10},{9,11},{10,... | collective-permute-start | bytes 1769480 | tf_op jit(solution)/shard_map/ppermute | solution.py:48
  35.9 23.2 %collective-permute-start.4 = (bf16[2,96,1536]{2,1,0:T(8,128)(2,1)S(1)}, bf16[2,96,1536]{2,1,0:T(8,128)(2,1)}, u32[]{:S(2)}, u32[]{:S(2)}) collective-permute-start(bf16[2,96,1536]{2,1,0:T(8,128)(2,1)S(1)} %pad_maximum_fusion.3.refs_0_), channel_id=1, source_target_pairs={{0,3},{1,0},{2,1},{3,2},{4,7},{5,4},{6,5},{7,6},{8,11},{9,8},{10,9... | collective-permute-start | bytes 1769480 | tf_op jit(solution)/shard_map/ppermute | solution.py:48
  59.1 10.9 %collective-permute-start.7 = (bf16[2,96,1536]{2,1,0:T(8,128)(2,1)S(1)}, bf16[2,96,1536]{2,1,0:T(8,128)(2,1)}, u32[]{:S(2)}, u32[]{:S(2)}) collective-permute-start(bf16[2,96,1536]{2,1,0:T(8,128)(2,1)S(1)} %collective-permute-done.1.refs_1_), channel_id=1, source_target_pairs={{0,8},{8,0},{16,24},{24,16},{32,40},{40,32},{48,56},{56,48},{64,72... | collective-permute-start | bytes 1769480 | tf_op jit(solution)/shard_map/ppermute | solution.py:38
  62.7 10.2 %collective-permute-start.8 = (bf16[2,96,1536]{2,1,0:T(8,128)(2,1)}, bf16[2,96,1536]{2,1,0:T(8,128)(2,1)}, u32[]{:S(2)}, u32[]{:S(2)}) collective-permute-start(bf16[2,96,1536]{2,1,0:T(8,128)(2,1)} %collective-permute-done.3.refs_2_), channel_id=1, source_target_pairs={{0,8},{8,0},{16,24},{24,16},{32,40},{40,32},{48,56},{56,48},{64,72... | collective-permute-start | bytes 1769480 | tf_op jit(solution)/shard_map/ppermute | solution.py:38
  70.0 57.0 %collective-permute-start.12 = (bf16[2,768,768]{2,1,0:T(8,128)(2,1)}, bf16[2,768,768]{2,1,0:T(8,128)(2,1)S(1)}, u32[]{:S(2)}, u32[]{:S(2)}) collective-permute-start(bf16[2,768,768]{2,1,0:T(8,128)(2,1)} %pad_maximum_fusion), channel_id=1, source_target_pairs={{0,120},{8,16},{16,8},{24,32},{32,24},{40,48},{48,40},{56,64},{64,... | collective-permute-start | bytes 7077896 | tf_op jit(solution)/shard_map/ppermute | solution.py:42
  123.5 55.9 %collective-permute-start.16 = (bf16[2,768,768]{2,1,0:T(8,128)(2,1)}, bf16[2,768,768]{2,1,0:T(8,128)(2,1)S(1)}, u32[]{:S(2)}, u32[]{:S(2)}) collective-permute-start(bf16[2,768,768]{2,1,0:T(8,128)(2,1)} %get-tuple-element.97), channel_id=1, source_target_pairs={{0,120},{8,16},{16,8},{24,32},{32,24},{40,48},{48,40},{56,64},{64,... | collective-permute-start | bytes 7077896 | tf_op jit(solution)/shard_map/ppermute | solution.py:42
  126.0 61.4 %collective-permute-start.15 = (bf16[2,768,768]{2,1,0:T(8,128)(2,1)S(1)}, bf16[2,768,768]{2,1,0:T(8,128)(2,1)}, u32[]{:S(2)}, u32[]{:S(2)}) collective-permute-start(bf16[2,768,768]{2,1,0:T(8,128)(2,1)S(1)} %get-tuple-element.94), channel_id=1, source_target_pairs={{0,8},{8,0},{16,24},{24,16},{32,40},{40,32},{48,56},{56,48},{64,72... | collective-permute-start | bytes 7077896 | tf_op jit(solution)/shard_map/ppermute | solution.py:38
  172.2 10.2 %collective-permute-start.14 = (bf16[8,96,768]{2,1,0:T(8,128)(2,1)S(1)}, bf16[8,96,768]{2,1,0:T(8,128)(2,1)S(1)}, u32[]{:S(2)}, u32[]{:S(2)}) collective-permute-start(bf16[8,96,768]{2,1,0:T(8,128)(2,1)S(1)} %get-tuple-element.91), channel_id=1, source_target_pairs={{0,8},{8,0},{16,24},{24,16},{32,40},{40,32},{48,56},{56,48},{64,72... | collective-permute-start | bytes 3538952 | tf_op jit(solution)/shard_map/ppermute | solution.py:38
  180.8 57.1 %collective-permute-start.27 = (bf16[2,768,768]{2,1,0:T(8,128)(2,1)}, bf16[2,768,768]{2,1,0:T(8,128)(2,1)S(1)}, u32[]{:S(2)}, u32[]{:S(2)}) collective-permute-start(bf16[2,768,768]{2,1,0:T(8,128)(2,1)} %copy-done.14), channel_id=1, source_target_pairs={{0,120},{8,16},{16,8},{24,32},{32,24},{40,48},{48,40},{56,64},{64,... | collective-permute-start | bytes 7077896 | tf_op jit(solution)/shard_map/ppermute | solution.py:42
  182.5 59.7 %collective-permute-start.13 = (bf16[2,768,768]{2,1,0:T(8,128)(2,1)}, bf16[2,768,768]{2,1,0:T(8,128)(2,1)}, u32[]{:S(2)}, u32[]{:S(2)}) collective-permute-start(bf16[2,768,768]{2,1,0:T(8,128)(2,1)} %copy-done.13), channel_id=1, source_target_pairs={{0,8},{8,0},{16,24},{24,16},{32,40},{40,32},{48,56},{56,48},{64,72... | collective-permute-start | bytes 7077896 | tf_op jit(solution)/shard_map/ppermute | solution.py:38
  185.4 10.7 %collective-permute-start.17 = (bf16[192,768]{1,0:T(8,128)(2,1)S(1)}, bf16[192,768]{1,0:T(8,128)(2,1)S(1)}, u32[]{:S(2)}, u32[]{:S(2)}) collective-permute-start(bf16[192,768]{1,0:T(8,128)(2,1)S(1)} %get-tuple-element.102), channel_id=1, source_target_pairs={{0,1},{1,2},{2,3},{3,0},{4,5},{5,6},{6,7},{7,4},{8,9},{9,10},{10,1... | collective-permute-start | bytes 884744 | tf_op jit(solution)/shard_map/ppermute | solution.py:48
  187.3 16.0 %collective-permute-start.18 = (bf16[192,768]{1,0:T(8,128)(2,1)S(1)}, bf16[192,768]{1,0:T(8,128)(2,1)S(1)}, u32[]{:S(2)}, u32[]{:S(2)}) collective-permute-start(bf16[192,768]{1,0:T(8,128)(2,1)S(1)} %get-tuple-element.103), channel_id=1, source_target_pairs={{0,2},{1,3},{2,0},{3,1},{4,6},{5,7},{6,4},{7,5},{8,10},{9,11},{10,... | collective-permute-start | bytes 884744 | tf_op jit(solution)/shard_map/ppermute | solution.py:48
  189.1 16.9 %collective-permute-start.19 = (bf16[192,768]{1,0:T(8,128)(2,1)S(1)}, bf16[192,768]{1,0:T(8,128)(2,1)S(1)}, u32[]{:S(2)}, u32[]{:S(2)}) collective-permute-start(bf16[192,768]{1,0:T(8,128)(2,1)S(1)} %get-tuple-element.104), channel_id=1, source_target_pairs={{0,3},{1,0},{2,1},{3,2},{4,7},{5,4},{6,5},{7,6},{8,11},{9,8},{10,9... | collective-permute-start | bytes 884744 | tf_op jit(solution)/shard_map/ppermute | solution.py:48
  196.8 19.4 %collective-permute-start.21 = (bf16[192,768]{1,0:T(8,128)(2,1)}, bf16[192,768]{1,0:T(8,128)(2,1)}, u32[]{:S(2)}, u32[]{:S(2)}) collective-permute-start(bf16[192,768]{1,0:T(8,128)(2,1)} %get-tuple-element.108), channel_id=1, source_target_pairs={{0,1},{1,2},{2,3},{3,0},{4,5},{5,6},{6,7},{7,4},{8,9},{9,10},{10,1... | collective-permute-start | bytes 884744 | tf_op jit(solution)/shard_map/ppermute | solution.py:48
  204.0 12.5 %collective-permute-start.22 = (bf16[192,768]{1,0:T(8,128)(2,1)}, bf16[192,768]{1,0:T(8,128)(2,1)}, u32[]{:S(2)}, u32[]{:S(2)}) collective-permute-start(bf16[192,768]{1,0:T(8,128)(2,1)} %get-tuple-element.109), channel_id=1, source_target_pairs={{0,2},{1,3},{2,0},{3,1},{4,6},{5,7},{6,4},{7,5},{8,10},{9,11},{10,... | collective-permute-start | bytes 884744 | tf_op jit(solution)/shard_map/ppermute | solution.py:48
  206.7 10.5 %collective-permute-start.23 = (bf16[192,768]{1,0:T(8,128)(2,1)}, bf16[192,768]{1,0:T(8,128)(2,1)}, u32[]{:S(2)}, u32[]{:S(2)}) collective-permute-start(bf16[192,768]{1,0:T(8,128)(2,1)} %get-tuple-element.110), channel_id=1, source_target_pairs={{0,3},{1,0},{2,1},{3,2},{4,7},{5,4},{6,5},{7,6},{8,11},{9,8},{10,9... | collective-permute-start | bytes 884744 | tf_op jit(solution)/shard_map/ppermute | solution.py:48
  220.4 11.7 %collective-permute-start.25 = (bf16[48,1536]{1,0:T(8,128)(2,1)}, bf16[48,1536]{1,0:T(8,128)(2,1)S(1)}, u32[]{:S(2)}, u32[]{:S(2)}) collective-permute-start(bf16[48,1536]{1,0:T(8,128)(2,1)} %get-tuple-element.113), channel_id=1, source_target_pairs={{0,64},{8,72},{16,80},{24,88},{32,96},{40,104},{48,112},{56,120},{... | collective-permute-start | bytes 442376 | tf_op jit(solution)/shard_map/ppermute | solution.py:56
  220.6 16.3 %collective-permute-start.24 = (bf16[48,1536]{1,0:T(8,128)(2,1)}, bf16[48,1536]{1,0:T(8,128)(2,1)S(1)}, u32[]{:S(2)}, u32[]{:S(2)}) collective-permute-start(bf16[48,1536]{1,0:T(8,128)(2,1)} %get-tuple-element.112), channel_id=1, source_target_pairs={{0,32},{8,40},{16,48},{24,56},{32,64},{40,72},{48,80},{56,88},{64,... | collective-permute-start | bytes 442376 | tf_op jit(solution)/shard_map/ppermute | solution.py:56
  238.0 9.2 %collective-permute-start.30 = (bf16[12,1536]{1,0:T(8,128)(2,1)S(1)}, bf16[12,1536]{1,0:T(8,128)(2,1)S(1)}, u32[]{:S(2)}, u32[]{:S(2)}) collective-permute-start(bf16[12,1536]{1,0:T(8,128)(2,1)S(1)} %get-tuple-element.125), channel_id=1, source_target_pairs={{0,20},{1,21},{2,22},{3,23},{4,16},{5,17},{6,18},{7,19},{8,28},{9,... | collective-permute-start | bytes 110600 | tf_op jit(solution)/shard_map/ppermute | solution.py:66
  (29 other events, 185.7 us)

commit v4 on v3

--- a/solution.py
+++ b/solution.py
@@ -225,7 +225,7 @@
 
 def finish(own, from_in, from_out, first, held):
     width = own.shape[2]
-    step = 256
+    step = 384 if width % 384 == 0 else 256
     pair = pl.BlockSpec((2, ROWS, step), lambda i: (0, 0, i))
     place = pl.BlockSpec((ROWS, step), lambda i: (0, first * HEAD // step + i))
     whole = jax.ShapeDtypeStruct((ROWS, FEATURES), BF16)
@@ -372,7 +372,7 @@
     x_low = dp // 4
     half = lax.dynamic_slice_in_dim(out_weight, core * 96, 96, 0)
     leaving = [outgoing(i) for i in range(len(GROUPS))]
-    other = x_low_swap(half)
+    other = jnp.concatenate((x_low_swap(half[:48]), x_flip(half[48:], 1, 1)), axis=0)
     leaving[0], other = together((leaving[0], other))
     arriving = [outer_swap(leaving[0])]
     both = jnp.stack((jnp.where(x_low == 0, half, other), jnp.where(x_low == 0, other, half)))

time: 249 us -> 246 us (0.988)
    ppermute x5, starting transfers between devices: 14.3 us -> 10.8 us  [outer_swap(): lax.ppermute(a, 'tm', [(i, (i + 1) % 16 if i % 2 else (i - 1) % 16) for i...]
    ppermute x5, waiting for transfers between devices: 12.6 us -> 15.8 us  [outer_swap(): lax.ppermute(a, 'tm', [(i, (i + 1) % 16 if i % 2 else (i - 1) % 16) for i...]
    ppermute x3 -> x4, starting transfers between devices: 4.17 us -> 7.09 us  [x_flip(): return lax.ppermute(a, ('tm', 'dp'), pairs)]
    ppermute x1, waiting for transfers between devices: 4.18 us -> 1.46 us  [x_low_swap(): return lax.ppermute(a, 'dp', [(i, (i + 4) % 8) for i in range(8)])]
  transfers between devices with their start and end apart: 31 -> 32, of which waited for: 16 -> 15; matrix products, arithmetic and copies ran while one was open for 6% -> 7% of each run, Pallas kernels for 46% -> 46%
where the time goes in v4:
time: 246 us; the launch traced here: 245 us
  Pallas kernels  112 us (46%)
  waiting for transfers between devices  62.4 us (25%)
  starting transfers between devices  39 us (16%)
  local copies, waits for them, and re-layouts  25.6 us (10%)
  other arithmetic  5.22 us (2%)
    pallas_call x3, Pallas kernels, attention(): pl.pallas_call(attention_kernel, grid=(heads,), out_shape=[jax.ShapeDtype...  76.6 us
    ppermute x9, waiting for transfers between devices, z_shift(): lax.ppermute(a, 'dp', [(i, i // 4 * 4 + (i + by) % 4) for i in range(8)])  28 us
    ppermute x9, starting transfers between devices, z_shift(): lax.ppermute(a, 'dp', [(i, i // 4 * 4 + (i + by) % 4) for i in range(8)])  17.2 us
    unnamed x45, local copies, waits for them, and re-layouts  16.8 us
    ppermute x5, waiting for transfers between devices, outer_swap(): lax.ppermute(a, 'tm', [(i, (i + 1) % 16 if i % 2 else (i - 1) % 16) for i...  15.8 us
    ppermute x3, waiting for transfers between devices, y_shift(): return lax.ppermute(a, 'tm', [(i, (i + 4 * by) % 16) for i in range(16)])  13.8 us
    ppermute x5, starting transfers between devices, outer_swap(): lax.ppermute(a, 'tm', [(i, (i + 1) % 16 if i % 2 else (i - 1) % 16) for i...  10.8 us
    pallas_call x2, Pallas kernels, weight_parts(): pl.pallas_call(weight_kernel, grid=(HALF // 256,), out_shape=[jax.ShapeDt...  10.7 us
  transfers between devices with their start and end apart: 32, of which 15 were waited for; matrix products, arithmetic and copies ran while one was open for 7% of the time, Pallas kernels for 46%

profile of v4, /device:TPU:0, one launch (start us, length us, event | category | flops | bytes accessed | tf_op | source)
XLA Modules:
  0.0 245.4 jit_solution(3346903583108616565)
XLA Ops:
  1.7 2.9 %collective-permute-start.1 = (bf16[48,1536]{1,0:T(8,128)(2,1)S(1)}, bf16[48,1536]{1,0:T(8,128)(2,1)S(1)}, u32[]{:S(2)}, u32[]{:S(2)}) collective-permute-start(bf16[48,1536]{1,0:T(8,128)(2,1)S(1)} %get-tuple-element.125), channel_id=1, source_target_pairs={{0,20},{1,21},{2,22},{3,23},{4,16},{5,17},{6,18},{7,19},{8,28},{9,... | collective-permute-start | bytes 442376 | tf_op jit(solution)/shard_map/ppermute | solution.py:66
  17.3 9.1 %collective-permute-done.2.refs_1_ = bf16[2,96,1536]{2,1,0:T(8,128)(2,1)S(1)} collective-permute-done((bf16[2,96,1536]{2,1,0:T(8,128)(2,1)S(1)}, bf16[2,96,1536]{2,1,0:T(8,128)(2,1)S(1)}, u32[]{:S(2)}, u32[]{:S(2)}) %collective-permute-start.2) | collective-permute-done | bytes 589856 | tf_op jit(solution)/shard_map/ppermute | solution.py:48
  28.7 6.9 %collective-permute-done.6.kvx = bf16[2,768,256]{2,1,0:T(8,128)(2,1)S(1)} collective-permute-done((bf16[2,768,256]{2,1,0:T(8,128)(2,1)S(1)}, bf16[2,768,256]{2,1,0:T(8,128)(2,1)S(1)}, u32[]{:S(2)}, u32[]{:S(2)}) %collective-permute-start.6) | collective-permute-done | bytes 786464 | tf_op jit(solution)/shard_map/ppermute | solution.py:42
  38.9 4.3 %copy.24 = bf16[1,768,1536]{1,2,0:T(8,128)(2,1)} copy(bf16[1,768,1536]{2,1,0:T(8,128)(2,1)} %param.11) | data formatting | bytes 4718592 | tf_op args[3]
  46.4 9.6 %collective-permute-done.5.refs_3_ = bf16[2,96,1536]{2,1,0:T(8,128)(2,1)} collective-permute-done((bf16[2,96,1536]{2,1,0:T(8,128)(2,1)S(1)}, bf16[2,96,1536]{2,1,0:T(8,128)(2,1)}, u32[]{:S(2)}, u32[]{:S(2)}) %collective-permute-start.5) | collective-permute-done | bytes 589856 | tf_op jit(solution)/shard_map/ppermute | solution.py:48
  59.8 8.4 %collective-permute-done.3.kvx = bf16[2,768,512]{2,1,0:T(8,128)(2,1)S(1)} collective-permute-done((bf16[2,768,512]{2,1,0:T(8,128)(2,1)}, bf16[2,768,512]{2,1,0:T(8,128)(2,1)S(1)}, u32[]{:S(2)}, u32[]{:S(2)}) %collective-permute-start.3) | collective-permute-done | bytes 1572896 | tf_op jit(solution)/shard_map/ppermute | solution.py:42
  68.6 2.4 collective-permute-start.13
  72.1 10.0 %project.1.g_ref = bf16[768,1536]{1,0:T(8,128)(2,1)} custom-call(s32[2]{0:T(128)S(1)} %pad_add_fusion.1.place_ref, bf16[768,1536]{1,0:T(8,128)(2,1)} %bitcast.59, bf16[2,96,1536]{2,1,0:T(8,128)(2,1)S(1)} %pad_maximum_fusion.3.refs_0_, bf16[2,96,1536]{2,1,0:T(8,128)(2,1)S(1)} %collective-permute-done.2.refs_1_, ...), custom_call_target="tpu_custom_call" | custom-call | flops 1179648 | bytes 1000000 | tf_op jit(solution)/shard_map/project/pallas_call | solution.py:95
  82.1 13.9 %attention.3 = (bf16[768,1536]{1,0:T(8,128)(2,1)}, bf16[768,768]{1,0:T(8,128)(2,1)S(1)}, f32[2,768,768]{2,1,0:T(8,128)}, bf16[2,768,768]{2,1,0:T(8,128)(2,1)S(1)}, bf16[2,768,768]{2,1,0:T(8,128)(2,1)}) custom-call(s32[2,4]{1,0:T(2,128)S(1)} %get-tuple-element.130.codes_ref, s32[2,4]{1,0:T(2,128)S(1)} %select_reduce_fusion.lens_ref, ...), custom_call_target="tpu_custom_call" | custom-call | flops 28311552 | bytes 589824 | tf_op jit(solution)/shard_map/attention/pallas_call | solution.py:191
  95.9 25.6 %attention.4 = (bf16[768,1536]{1,0:T(8,128)(2,1)}, bf16[768,768]{1,0:T(8,128)(2,1)S(1)}, f32[2,768,768]{2,1,0:T(8,128)}, bf16[2,768,768]{2,1,0:T(8,128)(2,1)S(1)}, bf16[2,768,768]{2,1,0:T(8,128)(2,1)}) custom-call(s32[2,4]{1,0:T(2,128)S(1)} %get-tuple-element.130.codes_ref, ...), custom_call_target="tpu_custom_call", output_to_operand_aliasing={{0}: (9, {}), {1}: (10, {}), {2}: (11, {}), {3}: (12, {}), ... | custom-call | flops 56623104 | bytes 589824 | tf_op jit(solution)/shard_map/attention/pallas_call | solution.py:191
  121.6 3.2 %collective-permute-start.17 = (bf16[2,768,768]{2,1,0:T(8,128)(2,1)}, bf16[2,768,768]{2,1,0:T(8,128)(2,1)S(1)}, u32[]{:S(2)}, u32[]{:S(2)}) collective-permute-start(bf16[2,768,768]{2,1,0:T(8,128)(2,1)} %get-tuple-element.97), channel_id=1, source_target_pairs={{0,120},{8,16},{16,8},{24,32},{32,24},{40,48},{48,40},{56,64},{64,... | collective-permute-start | bytes 7077896 | tf_op jit(solution)/shard_map/ppermute | solution.py:42
  126.8 37.1 %attention.5 = (bf16[768,1536]{1,0:T(8,128)(2,1)}, bf16[768,768]{1,0:T(8,128)(2,1)S(1)}, f32[2,768,768]{2,1,0:T(8,128)}, bf16[2,768,768]{2,1,0:T(8,128)(2,1)S(1)}, bf16[2,768,768]{2,1,0:T(8,128)(2,1)S(1)}) custom-call(s32[2,4]{1,0:T(2,128)S(1)} %get-tuple-element.130.codes_ref, ...), custom_call_target="tpu_custom_call", output_to_operand_aliasing={{0}: (9, {})} | custom-call | flops 84934656 | bytes 589824 | tf_op jit(solution)/shard_map/attention/pallas_call | solution.py:191
  165.3 5.4 %weight_parts.2 = (f32[8,96,768]{2,1,0:T(8,128)S(1)}, bf16[8,96,768]{2,1,0:T(8,128)(2,1)S(1)}) custom-call(s32[1]{0:T(128)} %get-tuple-element.131.core_ref, bf16[1536,768]{1,0:T(8,128)(2,1)} %bitcast.56, bf16[768,768]{1,0:T(8,128)(2,1)S(1)} %get-tuple-element.89.att_ref), custom_call_target="tpu_custom_call" | custom-call | flops 589824 | bytes 500000 | tf_op jit(solution)/shard_map/weight_parts/pallas_call | solution.py:263
  171.3 5.3 %weight_parts.3 = (f32[8,96,768]{2,1,0:T(8,128)S(1)}, bf16[8,96,768]{2,1,0:T(8,128)(2,1)S(1)}) custom-call(s32[1]{0:T(128)} %get-tuple-element.131.core_ref, bf16[1536,768]{1,0:T(8,128)(2,1)} %bitcast.57, bf16[768,768]{1,0:T(8,128)(2,1)S(1)} %get-tuple-element.95.att_ref), custom_call_target="tpu_custom_call" | custom-call | flops 589824 | bytes 500000 | tf_op jit(solution)/shard_map/weight_parts/pallas_call | solution.py:263
  178.4 2.8 %collective-permute-start.28 = (bf16[2,768,768]{2,1,0:T(8,128)(2,1)}, bf16[2,768,768]{2,1,0:T(8,128)(2,1)S(1)}, u32[]{:S(2)}, u32[]{:S(2)}) collective-permute-start(bf16[2,768,768]{2,1,0:T(8,128)(2,1)} %copy-done.14), channel_id=1, source_target_pairs={{0,120},{8,16},{16,8},{24,32},{32,24},{40,48},{48,40},{56,64},{64,... | collective-permute-start | bytes 7077896 | tf_op jit(solution)/shard_map/ppermute | solution.py:42
  190.5 2.5 %core_sum.3 = (f32[192,768]{1,0:T(8,128)S(1)}, bf16[192,768]{1,0:T(8,128)(2,1)}, bf16[192,768]{1,0:T(8,128)(2,1)}, bf16[192,768]{1,0:T(8,128)(2,1)}) custom-call(s32[1]{0:T(128)} %get-tuple-element.132.z_ref, f32[8,96,768]{2,1,0:T(8,128)S(1)} %get-tuple-element.105.keep_ref, bf16[8,96,768]{2,1,0:T(8,128)(2,1)S(1)} %collective-permute-done.21.got_ref), custom_call_target="tpu_custom_call" | custom-call | flops 589824 | bytes 500000 | tf_op jit(solution)/shard_map/core_sum/pallas_call | solution.py:297
  196.8 5.6 %collective-permute-done.19.refs_2_ = bf16[192,768]{1,0:T(8,128)(2,1)S(1)} collective-permute-done((bf16[192,768]{1,0:T(8,128)(2,1)S(1)}, bf16[192,768]{1,0:T(8,128)(2,1)S(1)}, u32[]{:S(2)}, u32[]{:S(2)}) %collective-permute-start.19) | collective-permute-done | bytes 294944 | tf_op jit(solution)/shard_map/ppermute | solution.py:48
  205.6 2.6 %collective-permute-start.24 = (bf16[192,768]{1,0:T(8,128)(2,1)}, bf16[192,768]{1,0:T(8,128)(2,1)}, u32[]{:S(2)}, u32[]{:S(2)}) collective-permute-start(bf16[192,768]{1,0:T(8,128)(2,1)} %get-tuple-element.110), channel_id=1, source_target_pairs={{0,3},{1,0},{2,1},{3,2},{4,7},{5,4},{6,5},{7,6},{8,11},{9,8},{10,9... | collective-permute-start | bytes 884744 | tf_op jit(solution)/shard_map/ppermute | solution.py:48
  209.9 4.4 %finish.2 = (bf16[768,1536]{1,0:T(8,128)(2,1)}, bf16[768,1536]{1,0:T(8,128)(2,1)}) custom-call(f32[2,768,768]{2,1,0:T(8,128)} %get-tuple-element.93.own_ref, bf16[2,768,768]{2,1,0:T(8,128)(2,1)} %collective-permute-done.16.in_ref, bf16[2,768,768]{2,1,0:T(8,128)(2,1)S(1)} %copy-done.3), custom_call_target="tpu_custom_call" | custom-call | flops 589824 | bytes 589824 | tf_op jit(solution)/shard_map/finish/pallas_call | solution.py:233
  221.3 3.3 %collective-permute-done.27 = bf16[48,1536]{1,0:T(8,128)(2,1)S(1)} collective-permute-done((bf16[48,1536]{1,0:T(8,128)(2,1)}, bf16[48,1536]{1,0:T(8,128)(2,1)S(1)}, u32[]{:S(2)}, u32[]{:S(2)}) %collective-permute-start.27) | collective-permute-done | bytes 147488 | tf_op jit(solution)/shard_map/ppermute | solution.py:56
  224.6 6.4 %collective-permute-done.26 = bf16[48,1536]{1,0:T(8,128)(2,1)S(1)} collective-permute-done((bf16[48,1536]{1,0:T(8,128)(2,1)}, bf16[48,1536]{1,0:T(8,128)(2,1)S(1)}, u32[]{:S(2)}, u32[]{:S(2)}) %collective-permute-start.26) | collective-permute-done | bytes 147488 | tf_op jit(solution)/shard_map/ppermute | solution.py:56
  231.0 4.1 %collective-permute-done.25 = bf16[48,1536]{1,0:T(8,128)(2,1)S(1)} collective-permute-done((bf16[48,1536]{1,0:T(8,128)(2,1)}, bf16[48,1536]{1,0:T(8,128)(2,1)S(1)}, u32[]{:S(2)}, u32[]{:S(2)}) %collective-permute-start.25) | collective-permute-done | bytes 147488 | tf_op jit(solution)/shard_map/ppermute | solution.py:56
  236.3 3.1 %collective-permute-start.30 = (bf16[12,1536]{1,0:T(8,128)(2,1)S(1)}, bf16[12,1536]{1,0:T(8,128)(2,1)S(1)}, u32[]{:S(2)}, u32[]{:S(2)}) collective-permute-start(bf16[12,1536]{1,0:T(8,128)(2,1)S(1)} %get-tuple-element.128), channel_id=1, source_target_pairs={{0,16},{1,17},{2,18},{3,19},{4,20},{5,21},{6,22},{7,23},{8,24},{9,... | collective-permute-start | bytes 110600 | tf_op jit(solution)/shard_map/ppermute | solution.py:66
  240.4 4.4 %finish.3 = (bf16[768,1536]{1,0:T(8,128)(2,1)}, bf16[768,1536]{1,0:T(8,128)(2,1)}) custom-call(f32[2,768,768]{2,1,0:T(8,128)} %get-tuple-element.84.own_ref, bf16[2,768,768]{2,1,0:T(8,128)(2,1)} %collective-permute-done.14.in_ref, bf16[2,768,768]{2,1,0:T(8,128)(2,1)S(1)} %collective-permute-done.28.out_ref, ...), custom_call_target="tpu_custom_call", output_to_operand_aliasing={{0}: (3, {}), {1}: (4, {})} | custom-call | flops 589824 | bytes 589824 | tf_op jit(solution)/shard_map/finish/pallas_call | solution.py:233
  (118 shorter events, 60.9 us)
Async XLA Ops:
  4.9 77.2 %collective-permute-start.11 = (bf16[768,1536]{1,0:T(8,128)(2,1)}, bf16[768,1536]{1,0:T(8,128)(2,1)}, u32[]{:S(2)}, u32[]{:S(2)}) collective-permute-start(bf16[768,1536]{1,0:T(8,128)(2,1)} %bitcast.39), channel_id=1, source_target_pairs={{0,8},{8,0},{16,24},{24,16},{32,40},{40,32},{48,56},{56,48},{64,72... | collective-permute-start | bytes 7077896 | tf_op jit(solution)/shard_map/ppermute | solution.py:38
  4.9 77.2 %collective-permute-start.12 = (bf16[768,1536]{1,0:T(8,128)(2,1)}, bf16[768,1536]{1,0:T(8,128)(2,1)}, u32[]{:S(2)}, u32[]{:S(2)}) collective-permute-start(bf16[768,1536]{1,0:T(8,128)(2,1)} %bitcast.46), channel_id=1, source_target_pairs={{0,8},{8,0},{16,24},{24,16},{32,40},{40,32},{48,56},{56,48},{64,72... | collective-permute-start | bytes 7077896 | tf_op jit(solution)/shard_map/ppermute | solution.py:38
  10.2 16.2 %collective-permute-start.2 = (bf16[2,96,1536]{2,1,0:T(8,128)(2,1)S(1)}, bf16[2,96,1536]{2,1,0:T(8,128)(2,1)S(1)}, u32[]{:S(2)}, u32[]{:S(2)}) collective-permute-start(bf16[2,96,1536]{2,1,0:T(8,128)(2,1)S(1)} %pad_maximum_fusion.3.refs_0_), channel_id=1, source_target_pairs={{0,1},{1,2},{2,3},{3,0},{4,5},{5,6},{6,7},{7,4},{8,9},{9,10},{10,1... | collective-permute-start | bytes 1769480 | tf_op jit(solution)/shard_map/ppermute | solution.py:48
  12.2 23.5 %collective-permute-start.6 = (bf16[2,768,256]{2,1,0:T(8,128)(2,1)S(1)}, bf16[2,768,256]{2,1,0:T(8,128)(2,1)S(1)}, u32[]{:S(2)}, u32[]{:S(2)}) collective-permute-start(bf16[2,768,256]{2,1,0:T(8,128)(2,1)S(1)} %pad_maximum_fusion.2), channel_id=1, source_target_pairs={{0,120},{8,16},{16,8},{24,32},{32,24},{40,48},{48,40},{56,64},{64,... | collective-permute-start | bytes 2359304 | tf_op jit(solution)/shard_map/ppermute | solution.py:42
  26.4 41.8 %collective-permute-start.3 = (bf16[2,768,512]{2,1,0:T(8,128)(2,1)}, bf16[2,768,512]{2,1,0:T(8,128)(2,1)S(1)}, u32[]{:S(2)}, u32[]{:S(2)}) collective-permute-start(bf16[2,768,512]{2,1,0:T(8,128)(2,1)} %pad_maximum_fusion.1), channel_id=1, source_target_pairs={{0,120},{8,16},{16,8},{24,32},{32,24},{40,48},{48,40},{56,64},{64,... | collective-permute-start | bytes 4718600 | tf_op jit(solution)/shard_map/ppermute | solution.py:42
  27.4 19.0 %collective-permute-start.4 = (bf16[2,96,1536]{2,1,0:T(8,128)(2,1)S(1)}, bf16[2,96,1536]{2,1,0:T(8,128)(2,1)}, u32[]{:S(2)}, u32[]{:S(2)}) collective-permute-start(bf16[2,96,1536]{2,1,0:T(8,128)(2,1)S(1)} %pad_maximum_fusion.3.refs_0_), channel_id=1, source_target_pairs={{0,2},{1,3},{2,0},{3,1},{4,6},{5,7},{6,4},{7,5},{8,10},{9,11},{10,... | collective-permute-start | bytes 1769480 | tf_op jit(solution)/shard_map/ppermute | solution.py:48
  35.6 20.4 %collective-permute-start.5 = (bf16[2,96,1536]{2,1,0:T(8,128)(2,1)S(1)}, bf16[2,96,1536]{2,1,0:T(8,128)(2,1)}, u32[]{:S(2)}, u32[]{:S(2)}) collective-permute-start(bf16[2,96,1536]{2,1,0:T(8,128)(2,1)S(1)} %pad_maximum_fusion.3.refs_0_), channel_id=1, source_target_pairs={{0,3},{1,0},{2,1},{3,2},{4,7},{5,4},{6,5},{7,6},{8,11},{9,8},{10,9... | collective-permute-start | bytes 1769480 | tf_op jit(solution)/shard_map/ppermute | solution.py:48
  56.0 12.6 %collective-permute-start.8 = (bf16[2,96,1536]{2,1,0:T(8,128)(2,1)S(1)}, bf16[2,96,1536]{2,1,0:T(8,128)(2,1)}, u32[]{:S(2)}, u32[]{:S(2)}) collective-permute-start(bf16[2,96,1536]{2,1,0:T(8,128)(2,1)S(1)} %collective-permute-done.2.refs_1_), channel_id=1, source_target_pairs={{0,8},{8,0},{16,24},{24,16},{32,40},{40,32},{48,56},{56,48},{64,72... | collective-permute-start | bytes 1769480 | tf_op jit(solution)/shard_map/ppermute | solution.py:38
  59.6 11.4 %collective-permute-start.9 = (bf16[2,96,1536]{2,1,0:T(8,128)(2,1)}, bf16[2,96,1536]{2,1,0:T(8,128)(2,1)}, u32[]{:S(2)}, u32[]{:S(2)}) collective-permute-start(bf16[2,96,1536]{2,1,0:T(8,128)(2,1)} %collective-permute-done.4.refs_2_), channel_id=1, source_target_pairs={{0,8},{8,0},{16,24},{24,16},{32,40},{40,32},{48,56},{56,48},{64,72... | collective-permute-start | bytes 1769480 | tf_op jit(solution)/shard_map/ppermute | solution.py:38
  68.6 56.8 %collective-permute-start.13 = (bf16[2,768,768]{2,1,0:T(8,128)(2,1)}, bf16[2,768,768]{2,1,0:T(8,128)(2,1)S(1)}, u32[]{:S(2)}, u32[]{:S(2)}) collective-permute-start(bf16[2,768,768]{2,1,0:T(8,128)(2,1)} %pad_maximum_fusion), channel_id=1, source_target_pairs={{0,120},{8,16},{16,8},{24,32},{32,24},{40,48},{48,40},{56,64},{64,... | collective-permute-start | bytes 7077896 | tf_op jit(solution)/shard_map/ppermute | solution.py:42
  121.6 55.5 %collective-permute-start.17 = (bf16[2,768,768]{2,1,0:T(8,128)(2,1)}, bf16[2,768,768]{2,1,0:T(8,128)(2,1)S(1)}, u32[]{:S(2)}, u32[]{:S(2)}) collective-permute-start(bf16[2,768,768]{2,1,0:T(8,128)(2,1)} %get-tuple-element.97), channel_id=1, source_target_pairs={{0,120},{8,16},{16,8},{24,32},{32,24},{40,48},{48,40},{56,64},{64,... | collective-permute-start | bytes 7077896 | tf_op jit(solution)/shard_map/ppermute | solution.py:42
  124.8 61.4 %collective-permute-start.16 = (bf16[2,768,768]{2,1,0:T(8,128)(2,1)S(1)}, bf16[2,768,768]{2,1,0:T(8,128)(2,1)}, u32[]{:S(2)}, u32[]{:S(2)}) collective-permute-start(bf16[2,768,768]{2,1,0:T(8,128)(2,1)S(1)} %get-tuple-element.94), channel_id=1, source_target_pairs={{0,8},{8,0},{16,24},{24,16},{32,40},{40,32},{48,56},{56,48},{64,72... | collective-permute-start | bytes 7077896 | tf_op jit(solution)/shard_map/ppermute | solution.py:38
  170.7 10.6 %collective-permute-start.15 = (bf16[8,96,768]{2,1,0:T(8,128)(2,1)S(1)}, bf16[8,96,768]{2,1,0:T(8,128)(2,1)S(1)}, u32[]{:S(2)}, u32[]{:S(2)}) collective-permute-start(bf16[8,96,768]{2,1,0:T(8,128)(2,1)S(1)} %get-tuple-element.91), channel_id=1, source_target_pairs={{0,8},{8,0},{16,24},{24,16},{32,40},{40,32},{48,56},{56,48},{64,72... | collective-permute-start | bytes 3538952 | tf_op jit(solution)/shard_map/ppermute | solution.py:38
  178.4 9.8 %collective-permute-start.21 = (bf16[8,96,768]{2,1,0:T(8,128)(2,1)S(1)}, bf16[8,96,768]{2,1,0:T(8,128)(2,1)S(1)}, u32[]{:S(2)}, u32[]{:S(2)}) collective-permute-start(bf16[8,96,768]{2,1,0:T(8,128)(2,1)S(1)} %get-tuple-element.106), channel_id=1, source_target_pairs={{0,8},{8,0},{16,24},{24,16},{32,40},{40,32},{48,56},{56,48},{64,72... | collective-permute-start | bytes 3538952 | tf_op jit(solution)/shard_map/ppermute | solution.py:38
  178.4 57.7 %collective-permute-start.28 = (bf16[2,768,768]{2,1,0:T(8,128)(2,1)}, bf16[2,768,768]{2,1,0:T(8,128)(2,1)S(1)}, u32[]{:S(2)}, u32[]{:S(2)}) collective-permute-start(bf16[2,768,768]{2,1,0:T(8,128)(2,1)} %copy-done.14), channel_id=1, source_target_pairs={{0,120},{8,16},{16,8},{24,32},{32,24},{40,48},{48,40},{56,64},{64,... | collective-permute-start | bytes 7077896 | tf_op jit(solution)/shard_map/ppermute | solution.py:42
  181.3 59.1 %collective-permute-start.14 = (bf16[2,768,768]{2,1,0:T(8,128)(2,1)}, bf16[2,768,768]{2,1,0:T(8,128)(2,1)}, u32[]{:S(2)}, u32[]{:S(2)}) collective-permute-start(bf16[2,768,768]{2,1,0:T(8,128)(2,1)} %copy-done.13), channel_id=1, source_target_pairs={{0,8},{8,0},{16,24},{24,16},{32,40},{40,32},{48,56},{56,48},{64,72... | collective-permute-start | bytes 7077896 | tf_op jit(solution)/shard_map/ppermute | solution.py:38
  184.2 10.7 %collective-permute-start.18 = (bf16[192,768]{1,0:T(8,128)(2,1)S(1)}, bf16[192,768]{1,0:T(8,128)(2,1)S(1)}, u32[]{:S(2)}, u32[]{:S(2)}) collective-permute-start(bf16[192,768]{1,0:T(8,128)(2,1)S(1)} %get-tuple-element.102), channel_id=1, source_target_pairs={{0,1},{1,2},{2,3},{3,0},{4,5},{5,6},{6,7},{7,4},{8,9},{9,10},{10,1... | collective-permute-start | bytes 884744 | tf_op jit(solution)/shard_map/ppermute | solution.py:48
  186.2 16.2 %collective-permute-start.19 = (bf16[192,768]{1,0:T(8,128)(2,1)S(1)}, bf16[192,768]{1,0:T(8,128)(2,1)S(1)}, u32[]{:S(2)}, u32[]{:S(2)}) collective-permute-start(bf16[192,768]{1,0:T(8,128)(2,1)S(1)} %get-tuple-element.103), channel_id=1, source_target_pairs={{0,2},{1,3},{2,0},{3,1},{4,6},{5,7},{6,4},{7,5},{8,10},{9,11},{10,... | collective-permute-start | bytes 884744 | tf_op jit(solution)/shard_map/ppermute | solution.py:48
  188.3 16.6 %collective-permute-start.20 = (bf16[192,768]{1,0:T(8,128)(2,1)S(1)}, bf16[192,768]{1,0:T(8,128)(2,1)S(1)}, u32[]{:S(2)}, u32[]{:S(2)}) collective-permute-start(bf16[192,768]{1,0:T(8,128)(2,1)S(1)} %get-tuple-element.104), channel_id=1, source_target_pairs={{0,3},{1,0},{2,1},{3,2},{4,7},{5,4},{6,5},{7,6},{8,11},{9,8},{10,9... | collective-permute-start | bytes 884744 | tf_op jit(solution)/shard_map/ppermute | solution.py:48
  195.7 18.6 %collective-permute-start.22 = (bf16[192,768]{1,0:T(8,128)(2,1)}, bf16[192,768]{1,0:T(8,128)(2,1)}, u32[]{:S(2)}, u32[]{:S(2)}) collective-permute-start(bf16[192,768]{1,0:T(8,128)(2,1)} %get-tuple-element.108), channel_id=1, source_target_pairs={{0,1},{1,2},{2,3},{3,0},{4,5},{5,6},{6,7},{7,4},{8,9},{9,10},{10,1... | collective-permute-start | bytes 884744 | tf_op jit(solution)/shard_map/ppermute | solution.py:48
  203.1 12.3 %collective-permute-start.23 = (bf16[192,768]{1,0:T(8,128)(2,1)}, bf16[192,768]{1,0:T(8,128)(2,1)}, u32[]{:S(2)}, u32[]{:S(2)}) collective-permute-start(bf16[192,768]{1,0:T(8,128)(2,1)} %get-tuple-element.109), channel_id=1, source_target_pairs={{0,2},{1,3},{2,0},{3,1},{4,6},{5,7},{6,4},{7,5},{8,10},{9,11},{10,... | collective-permute-start | bytes 884744 | tf_op jit(solution)/shard_map/ppermute | solution.py:48
  205.6 10.5 %collective-permute-start.24 = (bf16[192,768]{1,0:T(8,128)(2,1)}, bf16[192,768]{1,0:T(8,128)(2,1)}, u32[]{:S(2)}, u32[]{:S(2)}) collective-permute-start(bf16[192,768]{1,0:T(8,128)(2,1)} %get-tuple-element.110), channel_id=1, source_target_pairs={{0,3},{1,0},{2,1},{3,2},{4,7},{5,4},{6,5},{7,6},{8,11},{9,8},{10,9... | collective-permute-start | bytes 884744 | tf_op jit(solution)/shard_map/ppermute | solution.py:48
  219.2 11.7 %collective-permute-start.26 = (bf16[48,1536]{1,0:T(8,128)(2,1)}, bf16[48,1536]{1,0:T(8,128)(2,1)S(1)}, u32[]{:S(2)}, u32[]{:S(2)}) collective-permute-start(bf16[48,1536]{1,0:T(8,128)(2,1)} %get-tuple-element.113), channel_id=1, source_target_pairs={{0,64},{8,72},{16,80},{24,88},{32,96},{40,104},{48,112},{56,120},{... | collective-permute-start | bytes 442376 | tf_op jit(solution)/shard_map/ppermute | solution.py:56
  219.2 15.9 %collective-permute-start.25 = (bf16[48,1536]{1,0:T(8,128)(2,1)}, bf16[48,1536]{1,0:T(8,128)(2,1)S(1)}, u32[]{:S(2)}, u32[]{:S(2)}) collective-permute-start(bf16[48,1536]{1,0:T(8,128)(2,1)} %get-tuple-element.112), channel_id=1, source_target_pairs={{0,32},{8,40},{16,48},{24,56},{32,64},{40,72},{48,80},{56,88},{64,... | collective-permute-start | bytes 442376 | tf_op jit(solution)/shard_map/ppermute | solution.py:56
  (30 other events, 194.2 us)
